TPU v7x, 256 devices: a whole 4x4x8 slice. The times are simulated.
256 devices in a mesh: dom: 64 (over z, y, x_hi), edge: 4 (over x_lo, core).
Axes of the slice: x: 4 (x_hi: 2, x_lo: 2; x = x_hi * 2 + x_lo), y: 4, z: 8, core: 2. Of those that a mesh axis runs over, the one named last changes fastest.
Arguments:
- coordinates: bfloat16 [3, 32768], P(None, 'dom'), may hold values from 0 to 1
- features: bfloat16 [32768, 128], P('dom'), may hold values from -6 to 6
- species: int32 [32768], P('dom'), may hold values from 0 to 88
- ghost_map: int32 [1664, 64], P('dom'), may hold values from 0 to 511
- edge_sender: int32 [2097152], P(('dom', 'edge')), may hold values from 0 to 2175
- edge_receiver: int32 [2097152], P(('dom', 'edge')), may hold values from 0 to 511, as said below
- edge_count: int32 [64], P('dom'), may hold values from 16384 to 32768, as said below
- w_up: bfloat16 [128, 128], replicated, may hold values from -0.5 to 0.5
- radial_one: float32 [8, 64], replicated, may hold values from -2 to 2
- radial_two: float32 [64, 64], replicated, may hold values from -0.75 to 0.75
- radial_three: float32 [64, 384], replicated, may hold values from -0.75 to 0.75
- read_mix: float32 [640, 128], replicated, may hold values from -0.25 to 0.25
- species_out: float32 [89, 128], replicated, may hold values from -0.5 to 0.5
Outputs:
- energies: float32 [32768], P(('dom', 'edge'))
- forces: float32 [3, 32768], P(None, ('dom', 'edge'))
- feature_grad: float32 [32768, 128], P(('dom', 'edge'))
Inputs may be any that keep to these rules, and one draw needn't show every extreme that they name: The valid edge slots of a subdomain are its first edge_count slots; in every draw some subdomain uses all 32768. `edge_receiver`: within each subdomain's 32768 slots every owned atom is the receiver of exactly 64 slots, in no particular order.
All inputs are finite; a program needn't handle non-finite values.
Results may differ from a plain program's by a relative error of at most 0.0029.
Values may be sent and summed in bfloat16 or wider, within the bound.
A program may use at most 128 MiB of HBM per device.

v0:
```python
import math

import jax
import jax.numpy as jnp
from jax import lax
from jax.sharding import PartitionSpec as P

SLOTS_ATOM = 64


HIGH = lax.Precision.HIGHEST


def passed_along(value, axis, steps):
    count = lax.axis_size(axis)
    pairs = [(source, (source + steps) % count) for source in range(count)]
    return lax.ppermute(value, axis, pairs)


def cube_side(device_count):
    grid_side = 1
    while grid_side * grid_side * grid_side < device_count:
        grid_side = grid_side + 1
    return grid_side


def offset_table():
    return [
        (first_axis, second_axis, third_axis)
        for first_axis in (-1, 0, 1)
        for second_axis in (-1, 0, 1)
        for third_axis in (-1, 0, 1)
        if (first_axis, second_axis, third_axis) != (0, 0, 0)
    ]


def shift_amount(offset, grid_side):
    return offset[0] * grid_side * grid_side + offset[1] * grid_side + offset[2]


def radial_part(squared, edge_valid, radial_one, radial_two, radial_three):
    basis_count = radial_one.shape[0]
    betas = 0.4 * 15.0 ** (jnp.arange(basis_count, dtype=jnp.float32) / (basis_count - 1))
    basis = jnp.exp(-squared[:, None] * betas[None, :])
    envelope = jnp.square(jnp.maximum(0.0, 1.0 - squared / 4.0)) * edge_valid
    hidden_one = jax.nn.silu(jnp.dot(basis, radial_one, precision=HIGH))
    hidden_two = jax.nn.silu(jnp.dot(hidden_one, radial_two, precision=HIGH))
    return jnp.dot(hidden_two, radial_three, precision=HIGH) * envelope[:, None]


def harmonics(relative, squared):
    along_x = relative[0]
    along_y = relative[1]
    along_z = relative[2]
    return jnp.stack(
        [
            jnp.ones_like(squared),
            along_x,
            along_y,
            along_z,
            along_x * along_y,
            along_y * along_z,
            along_x * along_z,
            along_x * along_x - squared / 3.0,
            along_y * along_y - squared / 3.0,
        ],
        axis=1,
    )


def block_messages(positions, features_all, senders, receivers, edge_valid, weights):
    pos_send = jnp.take(positions, senders, axis=1)
    pos_recv = jnp.take(positions, receivers, axis=1)
    relative = pos_send - pos_recv
    squared = jnp.sum(relative * relative, axis=0)
    radial = radial_part(squared, edge_valid, weights[0], weights[1], weights[2])
    channels = features_all.shape[1]
    degree_terms = (
        radial.reshape(-1, 3, channels) * jnp.take(features_all, senders, axis=0)[:, None, :]
    )
    spread = jnp.concatenate(
        [
            degree_terms[:, 0:1],
            jnp.repeat(degree_terms[:, 1:2], 3, axis=1),
            jnp.repeat(degree_terms[:, 2:3], 5, axis=1),
        ],
        axis=1,
    )
    message = spread * harmonics(relative, squared)[:, :, None]
    return message.reshape(-1, 9 * channels)


def edge_sums(positions, features_all, senders, receivers, edge_valid, weights, atom_count):
    edge_total = senders.shape[0]
    block_size = min(1024, edge_total)
    block_count = edge_total // block_size

    def step_block(accum, items):
        send_rows, recv_rows, keep_rows = items
        message = block_messages(positions, features_all, send_rows, recv_rows, keep_rows, weights)
        return (accum + jax.ops.segment_sum(message, recv_rows, num_segments=atom_count), None)

    initial = jnp.zeros((atom_count, 9 * features_all.shape[1]), jnp.float32)
    accum, _ = lax.scan(
        jax.checkpoint(step_block),
        initial,
        (
            senders.reshape(block_count, block_size),
            receivers.reshape(block_count, block_size),
            edge_valid.reshape(block_count, block_size),
        ),
    )
    return accum * (1.0 / math.sqrt(SLOTS_ATOM))


def readout(node_data, kinds, read_mix, species_out):
    channels = species_out.shape[1]
    blocks = node_data.reshape(-1, 9, channels)
    scalar = blocks[:, 0]
    vector_x = blocks[:, 1]
    vector_y = blocks[:, 2]
    vector_z = blocks[:, 3]
    comp_xy = blocks[:, 4]
    comp_yz = blocks[:, 5]
    comp_xz = blocks[:, 6]
    comp_xx = blocks[:, 7]
    comp_yy = blocks[:, 8]
    comp_zz = -comp_xx - comp_yy
    norm_one = vector_x * vector_x + vector_y * vector_y + vector_z * vector_z
    norm_two = (
        comp_xx * comp_xx
        + comp_yy * comp_yy
        + comp_zz * comp_zz
        + 2.0 * (comp_xy * comp_xy + comp_yz * comp_yz + comp_xz * comp_xz)
    )
    cubic_term = (
        comp_xx * vector_x * vector_x
        + comp_yy * vector_y * vector_y
        + comp_zz * vector_z * vector_z
        + 2.0
        * (
            comp_xy * vector_x * vector_y
            + comp_yz * vector_y * vector_z
            + comp_xz * vector_x * vector_z
        )
    )
    invariants = jnp.concatenate(
        [scalar, norm_one, norm_two, scalar * norm_one, cubic_term], axis=1
    )
    hidden = jax.nn.silu(jnp.dot(invariants, read_mix, precision=HIGH))
    onehot = (kinds[:, None] == jnp.arange(species_out.shape[0], dtype=jnp.int32)[None, :]).astype(
        jnp.float32
    )
    per_kind = jnp.dot(onehot, species_out, precision=HIGH)
    return jnp.sum(hidden * per_kind, axis=1)


def on_device(
    coordinates,
    features,
    species,
    ghost_map,
    edge_sender,
    edge_receiver,
    edge_count,
    w_up,
    radial_one,
    radial_two,
    radial_three,
    read_mix,
    species_out,
):
    atom_count = features.shape[0]
    channels = features.shape[1]
    slot_size = ghost_map.shape[1]
    edge_groups = lax.axis_size("edge")
    quarter = atom_count // edge_groups
    grid_side = cube_side(lax.axis_size("dom"))
    offsets = offset_table()
    hprime = jnp.dot(features, w_up, preferred_element_type=jnp.float32).astype(jnp.bfloat16)
    sent_rows = jnp.take(hprime, ghost_map, axis=0)
    sent_coords = jnp.take(coordinates, ghost_map, axis=1)
    ghost_rows = []
    ghost_coords = []
    for number, offset in enumerate(offsets):
        got_rows, got_coords = passed_along(
            (sent_rows[number], sent_coords[:, number]), "dom", shift_amount(offset, grid_side)
        )
        ghost_rows.append(got_rows.astype(jnp.float32))
        ghost_coords.append(
            got_coords.astype(jnp.float32) - jnp.array(offset, dtype=jnp.float32)[:, None]
        )
    pos_all = jnp.concatenate([coordinates.astype(jnp.float32)] + ghost_coords, axis=1)
    h_all = jnp.concatenate(
        [lax.optimization_barrier(hprime).astype(jnp.float32)] + ghost_rows, axis=0
    )
    edges_here = edge_sender.shape[0]
    weights = (radial_one, radial_two, radial_three)
    first_atom = lax.axis_index("edge") * quarter
    first_edge = lax.axis_index("edge") * edges_here
    edge_valid = (first_edge + jnp.arange(edges_here, dtype=jnp.int32) < edge_count[0]).astype(
        jnp.float32
    )

    def forward(positions, row_data):
        return edge_sums(
            positions, row_data, edge_sender, edge_receiver, edge_valid, weights, atom_count
        )

    partial_sums, pull_back = jax.vjp(forward, pos_all, h_all)
    node_total = lax.psum(partial_sums, "edge")

    def energy_whole(sums):
        return readout(sums, species, read_mix, species_out)

    energy_all, pull_read = jax.vjp(energy_whole, node_total)
    (node_grad,) = pull_read(jnp.ones_like(energy_all))
    energies = lax.dynamic_slice_in_dim(energy_all, first_atom, quarter)
    pos_grad, row_grad = pull_back(node_grad)
    own_pos = pos_grad[:, :atom_count]
    own_rows = row_grad[:atom_count]
    ghost_pos_grad = pos_grad[:, atom_count:].reshape(3, 26, slot_size)
    ghost_row_grad = row_grad[atom_count:].reshape(26, slot_size, channels)
    for number, offset in enumerate(offsets):
        back_rows, back_pos = passed_along(
            (ghost_row_grad[number], ghost_pos_grad[:, number]),
            "dom",
            -shift_amount(offset, grid_side),
        )
        own_rows = own_rows.at[ghost_map[number]].add(back_rows)
        own_pos = own_pos.at[:, ghost_map[number]].add(back_pos)
    grad_rows, grad_pos = (
        lax.psum_scatter(own_rows, "edge", scatter_dimension=0, tiled=True),
        lax.psum_scatter(own_pos, "edge", scatter_dimension=1, tiled=True),
    )
    forces = -grad_pos
    feature_grad = jnp.dot(grad_rows, w_up.astype(jnp.float32).T, precision=HIGH)
    return (energies, forces, feature_grad)


def solution(mesh):
    return jax.shard_map(
        on_device,
        mesh=mesh,
        in_specs=(
            P(None, "dom"),
            P("dom", None),
            P("dom"),
            P("dom", None),
            P(("dom", "edge")),
            P(("dom", "edge")),
            P("dom"),
            P(),
            P(),
            P(),
            P(),
            P(),
            P(),
        ),
        out_specs=(P(("dom", "edge")), P(None, ("dom", "edge")), P(("dom", "edge"), None)),
        check_vma=False,
    )
```

profile of v0, /device:TPU:3, one launch (start us, length us, event | category | flops | bytes accessed | tf_op | source)
XLA Modules:
  0.0 1601.6 jit_solution(8453190431508198345)
XLA Ops:
  14.4 9.1 collective-permute-start.26
  113.8 8.4 collective-permute-done.22
  200.3 8.9 collective-permute-start.25
  209.9 8.3 collective-permute-start
  291.4 381.2 %while.30 = (s32[]{:T(128)}, f32[512,1152]{1,0:T(8,128)S(1)}, s32[8,1024]{1,0:T(8,128)S(1)}, s32[8,1024]{1,0:T(8,128)S(1)}, f32[3,2176]{0,1:T(8,128)}, /*index=5...) while((s32[]{:T(128)}, f32[512,1152]{1,0:T(8,128)S(1)}, ...), condition=%wide.region_3.5_spmd.clone, body=%wide.region_0.4_spmd.clone.sunk | while | flops 364834816 | bytes 51612924 | solution.py:104
  327.2 11.8 scatter_fusion.2
  374.9 11.8 scatter_fusion.2
  422.5 11.8 scatter_fusion.2
  470.2 11.8 scatter_fusion.2
  517.8 11.8 scatter_fusion.2
  565.5 11.8 scatter_fusion.2
  613.1 11.8 scatter_fusion.2
  660.8 11.8 scatter_fusion.2
  679.0 100.7 %all-reduce.16.cloned.1.call-done = f32[512,9,128]{2,0,1:T(8,128)} async-done(((f32[512,9,128]{2,0,1:T(8,128)}), f32[512,9,128]{2,0,1:T(8,128)}) %all-reduce.16.cloned.1.call-update) | async-done | bytes 2359312 | tf_op jit(solution)/shard_map/psum | solution.py:211
  794.9 556.4 %while.29 = (s32[]{:T(128)}, f32[3,2176]{0,1:T(8,128)}, f32[2176,128]{1,0:T(8,128)}, f32[512,1152]{1,0:T(8,128)S(1)}, s32[8,1024]{1,0:T(8,128)S(1)}, /*index=5*/...) while((s32[]{:T(128)}, f32[3,2176]{0,1:T(8,128)}, ...), condition=%wide.region_16.19_spmd, body=%wide.region_6.18_spmd.sunk | while | flops 731405312 | bytes 94465880 | solution.py:104
  843.5 12.9 scatter_fusion
  913.0 12.9 scatter_fusion
  982.6 12.9 scatter_fusion
  1052.1 12.9 scatter_fusion
  1121.6 12.9 scatter_fusion
  1191.1 12.9 scatter_fusion
  1260.6 12.9 scatter_fusion
  1330.2 12.9 scatter_fusion
  1566.4 26.6 %reduce-scatter.5.cloned.1.call-done = f32[128,128]{1,0:T(8,128)} async-done(((f32[512,128]{1,0:T(8,128)}), f32[128,128]{1,0:T(8,128)}) %reduce-scatter.5.cloned.1.call-update) | async-done | bytes 65552 | tf_op jit(solution)/shard_map/reduce_scatter | solution.py:233
  (1378 shorter events, 1221.2 us)
Async XLA Ops:
  7.2 772.5 %all-reduce.16.cloned.1.call-start = ((), (), s32[]{:S(2)}) async-start(), calls=%async_computation.2 | async-start | bytes 4718592 | tf_op jit(solution)/shard_map/psum | solution.py:211
  14.4 210.7 %collective-permute-start.26 = (bf16[64,128]{1,0:T(8,128)(2,1)S(1)}, bf16[64,128]{1,0:T(8,128)(2,1)S(1)}, u32[]{:S(2)}, u32[]{:S(2)}) collective-permute-start(bf16[64,128]{1,0:T(8,128)(2,1)S(1)} %get-tuple-element.645), channel_id=1, source_target_pairs={{0,172},{4,176},{8,180},{12,184},{16,188},{20,192},{24,196},{28,20... | collective-permute-start | bytes 49160 | tf_op jit(solution)/shard_map/ppermute | solution.py:17
  23.5 206.4 %collective-permute-start.27 = (bf16[64,128]{1,0:T(8,128)(2,1)S(1)}, bf16[64,128]{1,0:T(8,128)(2,1)S(1)}, u32[]{:S(2)}, u32[]{:S(2)}) collective-permute-start(bf16[64,128]{1,0:T(8,128)(2,1)S(1)} %get-tuple-element.644), channel_id=1, source_target_pairs={{0,176},{4,180},{8,184},{12,188},{16,192},{20,196},{24,200},{28,20... | collective-permute-start | bytes 49160 | tf_op jit(solution)/shard_map/ppermute | solution.py:17
  25.7 207.7 %collective-permute-start.28 = (bf16[64,128]{1,0:T(8,128)(2,1)S(1)}, bf16[64,128]{1,0:T(8,128)(2,1)S(1)}, u32[]{:S(2)}, u32[]{:S(2)}) collective-permute-start(bf16[64,128]{1,0:T(8,128)(2,1)S(1)} %get-tuple-element.643), channel_id=1, source_target_pairs={{0,180},{4,184},{8,188},{12,192},{16,196},{20,200},{24,204},{28,20... | collective-permute-start | bytes 49160 | tf_op jit(solution)/shard_map/ppermute | solution.py:17
  27.6 207.1 %collective-permute-start.29 = (bf16[64,128]{1,0:T(8,128)(2,1)S(1)}, bf16[64,128]{1,0:T(8,128)(2,1)S(1)}, u32[]{:S(2)}, u32[]{:S(2)}) collective-permute-start(bf16[64,128]{1,0:T(8,128)(2,1)S(1)} %get-tuple-element.642), channel_id=1, source_target_pairs={{0,188},{4,192},{8,196},{12,200},{16,204},{20,208},{24,212},{28,21... | collective-permute-start | bytes 49160 | tf_op jit(solution)/shard_map/ppermute | solution.py:17
  218.9 20.5 %collective-permute-start.30 = (bf16[64,128]{1,0:T(8,128)(2,1)S(1)}, bf16[64,128]{1,0:T(8,128)(2,1)S(1)}, u32[]{:S(2)}, u32[]{:S(2)}) collective-permute-start(bf16[64,128]{1,0:T(8,128)(2,1)S(1)} %get-tuple-element.641), channel_id=1, source_target_pairs={{0,192},{4,196},{8,200},{12,204},{16,208},{20,212},{24,216},{28,22... | collective-permute-start | bytes 49160 | tf_op jit(solution)/shard_map/ppermute | solution.py:17
  233.4 15.4 collective-permute-start.33
  258.8 16.4 %collective-permute-start.44 = (bf16[64,128]{1,0:T(8,128)(2,1)S(1)}, bf16[64,128]{1,0:T(8,128)(2,1)S(1)}, u32[]{:S(2)}, u32[]{:S(2)}) collective-permute-start(bf16[64,128]{1,0:T(8,128)(2,1)S(1)} %get-tuple-element.627), channel_id=1, source_target_pairs={{0,48},{4,52},{8,56},{12,60},{16,64},{20,68},{24,72},{28,76},{32,8... | collective-permute-start | bytes 49160 | tf_op jit(solution)/shard_map/ppermute | solution.py:17
  269.6 15.4 collective-permute-start.47
  678.6 886.3 %reduce-scatter.3.cloned.1.call-start = ((), (), s32[]{:S(2)}) async-start(), calls=%async_computation.3 | async-start | bytes 327680 | tf_op jit(solution)/shard_map/reduce_scatter | solution.py:234
  1352.6 21.4 %collective-permute-start.52 = (f32[3,64]{0,1:T(8,128)S(1)}, f32[3,64]{0,1:T(8,128)S(1)}, u32[]{:S(2)}, u32[]{:S(2)}) collective-permute-start(f32[3,64]{0,1:T(8,128)S(1)} %get-tuple-element.619), channel_id=1, source_target_pairs={{0,84},{4,88},{8,92},{12,96},{16,100},{20,104},{24,108},{28,112},{... | collective-permute-start | bytes 2312 | tf_op jit(solution)/shard_map/ppermute | solution.py:17
  1362.9 79.7 %collective-permute-start.78 = (f32[64,128]{1,0:T(8,128)S(1)}, f32[64,128]{1,0:T(8,128)S(1)}, u32[]{:S(2)}, u32[]{:S(2)}) collective-permute-start(f32[64,128]{1,0:T(8,128)S(1)} %get-tuple-element.593), channel_id=1, source_target_pairs={{0,84},{4,88},{8,92},{12,96},{16,100},{20,104},{24,108},{28,112},{... | collective-permute-start | bytes 98312 | tf_op jit(solution)/shard_map/ppermute | solution.py:17
  1431.8 17.1 %collective-permute-start.79 = (f32[64,128]{1,0:T(8,128)S(1)}, f32[64,128]{1,0:T(8,128)S(1)}, u32[]{:S(2)}, u32[]{:S(2)}) collective-permute-start(f32[64,128]{1,0:T(8,128)S(1)} %get-tuple-element.592), channel_id=1, source_target_pairs={{0,80},{4,84},{8,88},{12,92},{16,96},{20,100},{24,104},{28,108},{3... | collective-permute-start | bytes 98312 | tf_op jit(solution)/shard_map/ppermute | solution.py:17
  1436.3 15.6 collective-permute-start.80
  1442.6 16.2 %collective-permute-start.83 = (f32[64,128]{1,0:T(8,128)S(1)}, f32[64,128]{1,0:T(8,128)S(1)}, u32[]{:S(2)}, u32[]{:S(2)}) collective-permute-start(f32[64,128]{1,0:T(8,128)S(1)} %get-tuple-element.588), channel_id=1, source_target_pairs={{0,60},{4,64},{8,68},{12,72},{16,76},{20,80},{24,84},{28,88},{32,9... | collective-permute-start | bytes 98312 | tf_op jit(solution)/shard_map/ppermute | solution.py:17
  1473.4 15.7 collective-permute-start.95
  1478.5 15.1 collective-permute-start.96
  1484.4 15.4 collective-permute-start.98
  1487.4 63.3 %collective-permute-start.99 = (f32[64,128]{1,0:T(8,128)S(1)}, f32[64,128]{1,0:T(8,128)S(1)}, u32[]{:S(2)}, u32[]{:S(2)}) collective-permute-start(f32[64,128]{1,0:T(8,128)S(1)} %get-tuple-element.572), channel_id=1, source_target_pairs={{0,192},{4,196},{8,200},{12,204},{16,208},{20,212},{24,216},{28,22... | collective-permute-start | bytes 98312 | tf_op jit(solution)/shard_map/ppermute | solution.py:17
  1489.1 62.6 %collective-permute-start.100 = (f32[64,128]{1,0:T(8,128)S(1)}, f32[64,128]{1,0:T(8,128)S(1)}, u32[]{:S(2)}, u32[]{:S(2)}) collective-permute-start(f32[64,128]{1,0:T(8,128)S(1)} %get-tuple-element.571), channel_id=1, source_target_pairs={{0,188},{4,192},{8,196},{12,200},{16,204},{20,208},{24,212},{28,21... | collective-permute-start | bytes 98312 | tf_op jit(solution)/shard_map/ppermute | solution.py:17
  1493.6 59.2 %collective-permute-start.101 = (f32[64,128]{1,0:T(8,128)S(1)}, f32[64,128]{1,0:T(8,128)S(1)}, u32[]{:S(2)}, u32[]{:S(2)}) collective-permute-start(f32[64,128]{1,0:T(8,128)S(1)} %get-tuple-element.570), channel_id=1, source_target_pairs={{0,180},{4,184},{8,188},{12,192},{16,196},{20,200},{24,204},{28,20... | collective-permute-start | bytes 98312 | tf_op jit(solution)/shard_map/ppermute | solution.py:17
  1497.6 56.2 %collective-permute-start.102 = (f32[64,128]{1,0:T(8,128)S(1)}, f32[64,128]{1,0:T(8,128)S(1)}, u32[]{:S(2)}, u32[]{:S(2)}) collective-permute-start(f32[64,128]{1,0:T(8,128)S(1)} %get-tuple-element.569), channel_id=1, source_target_pairs={{0,176},{4,180},{8,184},{12,188},{16,192},{20,196},{24,200},{28,20... | collective-permute-start | bytes 98312 | tf_op jit(solution)/shard_map/ppermute | solution.py:17
  1499.8 55.1 %collective-permute-start.103 = (f32[64,128]{1,0:T(8,128)S(1)}, f32[64,128]{1,0:T(8,128)S(1)}, u32[]{:S(2)}, u32[]{:S(2)}) collective-permute-start(f32[64,128]{1,0:T(8,128)S(1)} %get-tuple-element.568), channel_id=1, source_target_pairs={{0,172},{4,176},{8,180},{12,184},{16,188},{20,192},{24,196},{28,20... | collective-permute-start | bytes 98312 | tf_op jit(solution)/shard_map/ppermute | solution.py:17
  1528.5 64.4 %reduce-scatter.5.cloned.1.call-start = ((), (), s32[]{:S(2)}) async-start(), calls=%async_computation.4 | async-start | bytes 327680 | tf_op jit(solution)/shard_map/reduce_scatter | solution.py:233
  (291 other events, 5524.5 us)
Sparse Core Ops, SparseCore 0:
  678.7 100.9 all-reduce.15
  1528.7 36.1 reduce-scatter.2
  1567.6 25.3 reduce-scatter.4
where the time goes:
time: 1620 us; the launch traced here: 1600 us
  local copies, waits for them, and re-layouts  480 us (30%)
  other arithmetic  447 us (28%)
  starting transfers between devices  294 us (18%)
  waiting for transfers between devices  254 us (16%)
  matrix products  105 us (6%)
    ppermute x104, starting transfers between devices, passed_along(): return lax.ppermute(value, axis, pairs)  293 us
    ppermute x104, waiting for transfers between devices, passed_along(): return lax.ppermute(value, axis, pairs)  120 us
    add_any x8, other arithmetic, block_messages(): pos_send = jnp.take(positions, senders, axis=1)  103 us
    psum x1, waiting for transfers between devices, on_device(): node_total = lax.psum(partial_sums, 'edge')  101 us
    scatter-add x8, other arithmetic, step_block(): jax.ops.segment_sum(message, recv_rows, num_segments=atom_count)  94.3 us
    gather x16, local copies, waits for them, and re-layouts, step_block(): jax.ops.segment_sum(message, recv_rows, num_segments=atom_count)  94.2 us
    gather x24, local copies, waits for them, and re-layouts, block_messages(): pos_send = jnp.take(positions, senders, axis=1)  76.2 us
    gather x24, local copies, waits for them, and re-layouts, block_messages(): pos_recv = jnp.take(positions, receivers, axis=1)  76 us
  transfers between devices with their start and end apart: 107, of which 31 were waited for; matrix products, arithmetic and copies ran while one was open for 4% of the time, Pallas kernels for 0%

commit v1 on v0

v1 whole, which is shorter than its diff:
```python
import jax
import jax.numpy as jnp
from jax import lax
from jax.experimental import pallas as pl
from jax.experimental.pallas import tpu as pltpu
from jax.sharding import PartitionSpec as P

F32, BF16, I32 = jnp.float32, jnp.bfloat16, jnp.int32
HIGH = lax.Precision.HIGHEST
MESH = pl.DeviceIdType.MESH
VMEM_SPEC = pl.BlockSpec(memory_space=pltpu.VMEM)

CH = 128
ATOMS = 512
OWN = 128
RANKS = 64
SLOT = 64
NOFF = 26
PAIRS = NOFF // 2
QUART = 4
EDGE_ROWS = 64
GROUPS = 9
GROWS = 144
NE = 256
STEPS = OWN * RANKS // NE
BLK = 80
SENTINEL = 4095
LIMIT = 56 * 1024 * 1024

OFFSETS = [
    (a, b, c)
    for a in (-1, 0, 1)
    for b in (-1, 0, 1)
    for c in (-1, 0, 1)
    if (a, b, c) != (0, 0, 0)
]


def shifts(count):
    side = 1
    while side * side * side < count:
        side += 1
    return [o[0] * side * side + o[1] * side + o[2] for o in OFFSETS]


def mm(a, b):
    return lax.dot_general(a, b, (((1,), (0,)), ((), ())), preferred_element_type=F32)


def mm_nt(a, b):
    return lax.dot_general(a, b, (((1,), (1,)), ((), ())), preferred_element_type=F32)


def mm_high(a, b):
    return lax.dot_general(
        a, b, (((1,), (0,)), ((), ())), precision=HIGH, preferred_element_type=F32
    )


def split(x):
    hi = x.astype(BF16)
    return hi, (x - hi.astype(F32)).astype(BF16)


def weight_stack(w):
    hi, lo = split(w)
    return jnp.concatenate([hi, hi, lo], axis=1)


def value_stack(x):
    hi, lo = split(x)
    return jnp.concatenate([hi, lo, hi], axis=0)


def iota(shape, dim):
    return lax.broadcasted_iota(I32, shape, dim)


def pair_rows(gmap_ref, p):
    return jnp.concatenate([gmap_ref[2 * p : 2 * p + 1, :], gmap_ref[2 * p + 1 : 2 * p + 2, :]], axis=1)


def neighbours(dom_size, number, sign):
    me = lax.axis_index("dom")
    step = shifts(dom_size)[number] * sign
    return lax.rem(me + (step % dom_size), dom_size)


def greet(dom_size):
    barrier = pltpu.get_barrier_semaphore()
    quarter = lax.axis_index("edge")
    me = lax.axis_index("dom")
    for number in range(NOFF):
        there = neighbours(dom_size, number, 1)
        pl.semaphore_signal(barrier, inc=1, device_id=(there, quarter), device_id_type=MESH)
    for j in range(1, QUART):
        peer = lax.rem(quarter + j, QUART)
        pl.semaphore_signal(barrier, inc=1, device_id=(me, peer), device_id_type=MESH)
    return barrier


def exchange_kernel(
    dom_size,
    feat_ref, wup_ref, coord_ref, gmap_ref, snd_ref, rcv_ref, cnt_ref,
    slots_ref, blocks_ref, own_ref,
    sendblk, epack, li_s, g_s, hi_s, tri_s, send_sem, recv_sem,
):
    me = lax.axis_index("dom")
    quarter = lax.axis_index("edge")
    barrier = greet(dom_size)

    first = quarter * (EDGE_ROWS * 128)
    index = first + iota((EDGE_ROWS, 128), 0) * 128 + iota((EDGE_ROWS, 128), 1)
    sender = jnp.where(index < cnt_ref[0], snd_ref[...], SENTINEL)
    epack[quarter] = sender + rcv_ref[...] * 65536

    hprime = mm(feat_ref[...], wup_ref[...]).astype(BF16)
    h_t = hprime.astype(F32).T.astype(BF16)
    own_ref[...] = h_t
    coords = jnp.concatenate(
        [coord_ref[...].astype(F32), jnp.zeros((13, ATOMS), F32)], axis=0
    ).astype(BF16)
    ext = jnp.concatenate([h_t, coords], axis=0)

    pl.semaphore_wait(barrier, NOFF + QUART - 1)

    copies = []
    for j in range(1, QUART):
        peer = lax.rem(quarter + j, QUART)
        copy = pltpu.make_async_remote_copy(
            src_ref=epack.at[quarter],
            dst_ref=epack.at[quarter],
            send_sem=send_sem.at[NOFF + j - 1],
            recv_sem=recv_sem.at[NOFF + j - 1],
            device_id=(me, peer),
            device_id_type=MESH,
        )
        copy.start()
        copies.append(copy)

    low = iota((64, 128), 1) < 64
    low16 = iota((16, 128), 1) < 64
    ghosts = []
    for p in range(PAIRS):
        row = pair_rows(gmap_ref, p)
        onehot = jnp.where(iota((ATOMS, 128), 0) == row, 1.0, 0.0).astype(BF16)
        picked = mm(ext, onehot)
        top, bottom, pos = picked[0:64], picked[64:128], picked[128:144]
        even = jnp.where(low, top, pltpu.roll(bottom, 64, 1))
        odd = jnp.where(low, pltpu.roll(top, 64, 1), bottom)
        sendblk[2 * p, 0:64, :] = even.astype(BF16)
        sendblk[2 * p + 1, 0:64, :] = odd.astype(BF16)
        sendblk[2 * p, 64:80, :] = jnp.where(low16, pos, 0.0).astype(BF16)
        sendblk[2 * p + 1, 64:80, :] = jnp.where(low16, pltpu.roll(pos, 64, 1), 0.0).astype(BF16)
        for number in (2 * p, 2 * p + 1):
            copy = pltpu.make_async_remote_copy(
                src_ref=sendblk.at[number],
                dst_ref=blocks_ref.at[number],
                send_sem=send_sem.at[number],
                recv_sem=recv_sem.at[number],
                device_id=(neighbours(dom_size, number, 1), quarter),
                device_id_type=MESH,
            )
            copy.start()
            ghosts.append(copy)

    for copy in copies:
        copy.wait_recv()

    packed = epack[...].reshape(QUART * EDGE_ROWS, 128)
    local = (packed >> 16) - quarter * OWN
    inside = (local >= 0) & (local < OWN)
    li_s[...] = jnp.where(inside, local, 255).astype(F32)
    value = packed & 65535
    g_s[...] = (value >> 8).astype(F32)
    hi_s[...] = (value & 255).astype(F32)
    tri_s[:, 0:256] = jnp.where(iota((256, 256), 0) < iota((256, 256), 1), 1.0, 0.0).astype(BF16)
    tri_s[:, 256:384] = jnp.ones((256, 128), BF16)

    atom = iota((OWN, 256), 0).astype(F32)
    rank_of = iota((RANKS, 256), 0).astype(F32)

    def sort_step(step, carry):
        base, total = carry
        rows = pl.ds(pl.multiple_of(step * 8, 8), 8)
        li8, g8, hi8 = li_s[rows, :], g_s[rows, :], hi_s[rows, :]

        def lane_row(x, b):
            return jnp.concatenate([x[2 * b : 2 * b + 1], x[2 * b + 1 : 2 * b + 2]], axis=1)

        hots = [jnp.where(atom == lane_row(li8, b), 1.0, 0.0) for b in range(4)]
        hots16 = [hot.astype(BF16) for hot in hots]
        counts = mm(jnp.concatenate(hots16, axis=0), tri_s[...])
        lefts = []
        for b in range(4):
            block = counts[OWN * b : OWN * (b + 1)]
            before = block[:, 0:256] + jnp.concatenate([base, base], axis=1)
            base = base + block[:, 256:384]
            rank = jnp.sum(before * hots[b], axis=0, keepdims=True)
            here = rank_of == rank
            lefts.append(
                jnp.concatenate(
                    [
                        jnp.where(here, lane_row(g8, b), 0.0).astype(BF16),
                        jnp.where(here, lane_row(hi8, b), 0.0).astype(BF16),
                    ],
                    axis=0,
                )
            )
        total = total + mm_nt(jnp.concatenate(lefts, axis=1), jnp.concatenate(hots16, axis=1))
        return base, total

    zero = jnp.zeros((OWN, 128), F32)
    _, total = lax.fori_loop(0, QUART * EDGE_ROWS // 8, sort_step, (zero, zero))
    slots_ref[...] = (total[0:64] * 256.0 + total[64:128]).astype(I32)

    for copy in ghosts:
        copy.wait_recv()
    for copy in copies + ghosts:
        copy.wait_send()


def compute_kernel(
    slots_ref, blocks_ref, own_ref, coord_ref, species_ref,
    w1_ref, w2_ref, w3_ref, mix_ref, sp_ref,
    energy_ref, gblocks_ref, gown_ref,
    tab, hot_s, acc, rad_s, h_s, d1_s, d2_s, bas_s, row_s, scat, sp_s,
    w1f, w2f, w3f, w1b, w2b, w3b, myc,
):
    quarter = lax.axis_index("edge")
    lane = iota((64, 128), 1)
    low = lane < 64
    low8 = iota((8, 128), 1) < 64
    low16 = iota((16, 128), 1) < 64
    sub8 = iota((8, 128), 0)

    coords = coord_ref[...].astype(F32)
    coords16 = jnp.concatenate([coords, jnp.zeros((13, ATOMS), F32)], axis=0).astype(BF16)
    for g in range(2):
        tab[GROWS * g : GROWS * g + 128, :] = own_ref[:, 256 * g : 256 * g + 256]
        tab[GROWS * g + 128 : GROWS * (g + 1), :] = coords16[:, 256 * g : 256 * g + 256]
    tab[GROWS * 8 : GROWS * 9, :] = jnp.zeros((GROWS, 256), BF16)
    for p in range(PAIRS):
        g, at = 2 + p // 2, 128 * (p % 2)
        even = blocks_ref[2 * p].astype(F32)
        odd = blocks_ref[2 * p + 1].astype(F32)
        top = jnp.where(low, even[0:64], pltpu.roll(odd[0:64], 64, 1))
        bottom = jnp.where(low, pltpu.roll(even[0:64], 64, 1), odd[0:64])
        pos = jnp.where(low16, even[64:80], pltpu.roll(odd[64:80], 64, 1))
        oe, oo = OFFSETS[2 * p], OFFSETS[2 * p + 1]
        off = jnp.zeros((16, 128), F32)
        sub16 = iota((16, 128), 0)
        for c in range(3):
            if oe[c] != 0 or oo[c] != 0:
                off = jnp.where(sub16 == 3 + c, jnp.where(low16, float(oe[c]), float(oo[c])), off)
        pos = pos + off
        tab[GROWS * g : GROWS * g + 64, at : at + 128] = top.astype(BF16)
        tab[GROWS * g + 64 : GROWS * g + 128, at : at + 128] = bottom.astype(BF16)
        tab[GROWS * g + 128 : GROWS * (g + 1), at : at + 128] = pos.astype(BF16)

    w1f[...] = weight_stack(w1_ref[...].T)
    w2f[...] = weight_stack(w2_ref[...].T)
    w3f[...] = weight_stack(w3_ref[...].T)
    w1b[...] = weight_stack(w1_ref[...])
    w2b[...] = weight_stack(w2_ref[...])
    hi, lo = split(w3_ref[...])
    w3b[...] = jnp.concatenate([hi, lo], axis=0)

    acc[...] = jnp.zeros(acc.shape, F32)
    scat[...] = jnp.zeros(scat.shape, F32)
    mine = pl.ds(pl.multiple_of(quarter * OWN, OWN), OWN)
    my_coords = coord_ref[:, mine].astype(F32)
    for c in range(3):
        mc = jnp.broadcast_to(my_coords[c : c + 1], (8, 128))
        myc[8 * c : 8 * c + 8, :] = jnp.concatenate([mc, mc], axis=1)

    beta = jnp.zeros((8, NE), F32)
    for n in range(8):
        beta = jnp.where(iota((8, NE), 0) == n, 0.4 * 15.0 ** (n / 7.0), beta)

    def slot_row(step):
        s = jnp.concatenate(
            [slots_ref[pl.ds(2 * step, 1), :], slots_ref[pl.ds(2 * step + 1, 1), :]], axis=1
        )
        return jnp.broadcast_to(s, (8, NE))

    def harmonic(x, y, z, dsq):
        third = dsq * (1.0 / 3.0)
        return [None, x, y, z, x * y, y * z, x * z, x * x - third, y * y - third]

    degree = [0, 1, 1, 1, 2, 2, 2, 2, 2]

    def fwd(step, carry):
        lanes = pl.ds(pl.multiple_of(step * NE, NE), NE)
        s = slot_row(step)
        group = s >> 8
        hi = s & 255
        valid = jnp.where(group < GROUPS, 1.0, 0.0)
        sub = iota((8, NE), 0)
        onehot = jnp.concatenate(
            [jnp.where(sub + 8 * t == hi, 1.0, 0.0) for t in range(32)], axis=0
        ).astype(BF16)
        hot_s[:, lanes] = onehot
        got = mm(tab[...], onehot)
        masks = [group == k for k in range(GROUPS)]
        rows = []
        for t in range(17):
            v = jnp.zeros((8, NE), F32)
            for k in range(GROUPS):
                at = GROWS * k + 8 * t
                v = jnp.where(masks[k], got[at : at + 8], v)
            rows.append(v)
        pos = rows[16]
        rel = []
        for c in range(3):
            sent = pos[c : c + 1] - pos[3 + c : 4 + c]
            rel.append(jnp.broadcast_to(sent, (8, NE)) - myc[8 * c : 8 * c + 8, :])
        x, y, z = rel
        dsq = x * x + y * y + z * z
        e0 = jnp.maximum(0.0, 1.0 - dsq * 0.25) * valid
        env = e0 * e0
        basis = jnp.exp(-dsq * beta)
        packed = jnp.zeros((8, NE), F32)
        for j, v in enumerate((x, y, z, dsq, env, e0)):
            packed = jnp.where(sub == j, v, packed)
        row_s[:, lanes] = packed
        bas_s[:, lanes] = basis

        def act(pre):
            sig = 0.5 + 0.5 * jnp.tanh(0.5 * pre)
            out = pre * sig
            return out, sig + out * (1.0 - sig)

        h1, d1 = act(mm(w1f[...], value_stack(basis)))
        d1_s[:, lanes] = d1
        h2, d2 = act(mm(w2f[...], value_stack(h1)))
        d2_s[:, lanes] = d2
        rad = mm(w3f[...], value_stack(h2))
        rad_s[:, lanes] = rad
        ys = harmonic(x, y, z, dsq)
        for t in range(16):
            h = rows[t]
            h_s[8 * t : 8 * t + 8, lanes] = h
            he = h * env
            ds = [he * rad[128 * l + 8 * t : 128 * l + 8 * t + 8] for l in range(3)]
            for m in range(9):
                msg = ds[degree[m]] if m == 0 else ds[degree[m]] * ys[m]
                at = 128 * m + 8 * t
                acc[at : at + 8, :] += msg[:, 0:128] + msg[:, 128:256]
        return carry

    lax.fori_loop(0, STEPS, fwd, 0)

    def node(m):
        return acc[128 * m : 128 * m + 128, :] * 0.125

    a0, vx, vy, vz, xy, yz, xz, xx, yy = [node(m) for m in range(9)]
    zz = -xx - yy
    n1 = vx * vx + vy * vy + vz * vz
    n2 = xx * xx + yy * yy + zz * zz + 2.0 * (xy * xy + yz * yz + xz * xz)
    cx = xx * vx + xy * vy + xz * vz
    cy = xy * vx + yy * vy + yz * vz
    cz = xz * vx + yz * vy + zz * vz
    cub = cx * vx + cy * vy + cz * vz
    inv = jnp.concatenate([a0, n1, n2, a0 * n1, cub], axis=0)
    pre = mm_high(mix_ref[...].T, inv)
    sig = 0.5 + 0.5 * jnp.tanh(0.5 * pre)
    hid = pre * sig
    sp_s[...] = jnp.zeros((128, 128), F32)
    sp_s[0:89, :] = sp_ref[...]
    kinds = species_ref[pl.ds(quarter, 1), :]
    kind_hot = jnp.where(iota((128, 128), 0) == kinds, 1.0, 0.0)
    per_kind = mm_high(sp_s[...].T, kind_hot)
    energy_ref[...] = jnp.sum(hid * per_kind, axis=0, keepdims=True)
    dpre = per_kind * (sig + hid * (1.0 - sig))
    dinv = mm_high(mix_ref[...], dpre) * 0.125
    g0, g1, g2, g3, g4 = [dinv[128 * j : 128 * j + 128] for j in range(5)]
    w = 2.0 * (g1 + g3 * a0)
    c2 = 2.0 * g4
    acc[0:128, :] = g0 + g3 * n1
    acc[128:256, :] = w * vx + c2 * cx
    acc[256:384, :] = w * vy + c2 * cy
    acc[384:512, :] = w * vz + c2 * cz
    acc[512:640, :] = 4.0 * xy * g2 + c2 * vx * vy
    acc[640:768, :] = 4.0 * yz * g2 + c2 * vy * vz
    acc[768:896, :] = 4.0 * xz * g2 + c2 * vx * vz
    acc[896:1024, :] = 2.0 * g2 * (xx - zz) + g4 * (vx * vx - vz * vz)
    acc[1024:1152, :] = 2.0 * g2 * (yy - zz) + g4 * (vy * vy - vz * vz)

    def bwd(step, down):
        lanes = pl.ds(pl.multiple_of(step * NE, NE), NE)
        group = slot_row(step) >> 8
        rows = row_s[:, lanes]
        x, y, z, dsq, env, e0 = [jnp.broadcast_to(rows[j : j + 1], (8, NE)) for j in range(6)]
        ys = harmonic(x, y, z, dsq)
        denv = jnp.zeros((8, NE), F32)
        dys = [jnp.zeros((8, NE), F32) for _ in range(9)]
        dhs, drs = [], [[], [], []]
        for t in range(16):
            da = []
            for m in range(9):
                v = acc[128 * m + 8 * t : 128 * m + 8 * t + 8, :]
                da.append(jnp.concatenate([v, v], axis=1))
            t0 = da[0]
            t1 = x * da[1] + y * da[2] + z * da[3]
            t2 = ys[4] * da[4]
            for m in range(5, 9):
                t2 = t2 + ys[m] * da[m]
            ts = [t0, t1, t2]
            rs = [rad_s[128 * l + 8 * t : 128 * l + 8 * t + 8, lanes] for l in range(3)]
            u = rs[0] * t0 + rs[1] * t1 + rs[2] * t2
            h = h_s[8 * t : 8 * t + 8, lanes]
            he = h * env
            denv = denv + h * u
            dhs.append(env * u)
            for l in range(3):
                drs[l].append(he * ts[l])
            d1, d2 = he * rs[1], he * rs[2]
            for m in range(1, 9):
                dys[m] = dys[m] + (d1 if m < 4 else d2) * da[m]

        def total(v):
            return jnp.broadcast_to(jnp.sum(v, axis=0, keepdims=True), (8, NE))

        drad = jnp.concatenate(drs[0] + drs[1] + drs[2], axis=0).astype(BF16)
        both = mm(w3b[...], drad)
        dp2 = (both[0:64] + both[64:128]) * d2_s[:, lanes]
        dp1 = mm(w2b[...], value_stack(dp2)) * d1_s[:, lanes]
        dbas = mm(w1b[...], value_stack(dp1))
        denv = total(denv)
        dys = [None] + [total(v) for v in dys[1:]]
        ddsq = (
            -total(dbas * bas_s[:, lanes] * beta)
            - 0.5 * e0 * denv
            - (dys[7] + dys[8]) * (1.0 / 3.0)
        )
        two = 2.0 * ddsq
        dx = dys[1] + y * dys[4] + z * dys[6] + 2.0 * x * dys[7] + x * two
        dy = dys[2] + x * dys[4] + z * dys[5] + 2.0 * y * dys[8] + y * two
        dz = dys[3] + y * dys[5] + x * dys[6] + z * two
        sub = iota((8, NE), 0)
        drel = jnp.where(sub == 0, dx, jnp.where(sub == 1, dy, jnp.where(sub == 2, dz, 0.0)))
        drel_hi = drel.astype(BF16).astype(F32)
        flow = jnp.concatenate(dhs + [drel_hi, drel - drel_hi], axis=0).astype(BF16)
        group16 = jnp.concatenate([group, group], axis=0)
        lefts = []
        for k in range(GROUPS):
            mask = jnp.where(group16 == k, 1.0, 0.0).astype(BF16)
            lefts.extend(flow[16 * t : 16 * t + 16] * mask for t in range(9))
        scat[...] += mm_nt(jnp.concatenate(lefts, axis=0), hot_s[:, lanes])
        return down + drel[:, 0:128] + drel[:, 128:256]

    down = lax.fori_loop(0, STEPS, bwd, jnp.zeros((8, 128), F32))

    for g in range(2):
        span = slice(256 * g, 256 * g + 256)
        gown_ref[0:128, span] = scat[GROWS * g : GROWS * g + 128, :]
        gown_ref[128:136, span] = (
            scat[GROWS * g + 128 : GROWS * g + 136, :] + scat[GROWS * g + 136 : GROWS * g + 144, :]
        )
    gown_ref[128:136, mine] = gown_ref[128:136, mine] - down
    for p in range(PAIRS):
        g, at = 2 + p // 2, 128 * (p % 2)
        top = scat[GROWS * g : GROWS * g + 64, at : at + 128]
        bottom = scat[GROWS * g + 64 : GROWS * g + 128, at : at + 128]
        pos = (
            scat[GROWS * g + 128 : GROWS * g + 136, at : at + 128]
            + scat[GROWS * g + 136 : GROWS * g + 144, at : at + 128]
        )
        pos_hi = pos.astype(BF16).astype(F32)
        pos = jnp.concatenate([pos_hi, pos - pos_hi], axis=0)
        even = jnp.where(low, top, pltpu.roll(bottom, 64, 1))
        odd = jnp.where(low, pltpu.roll(top, 64, 1), bottom)
        gblocks_ref[2 * p, 0:64, :] = even.astype(BF16)
        gblocks_ref[2 * p + 1, 0:64, :] = odd.astype(BF16)
        gblocks_ref[2 * p, 64:80, :] = jnp.where(low16, pos, 0.0).astype(BF16)
        gblocks_ref[2 * p + 1, 64:80, :] = jnp.where(low16, pltpu.roll(pos, 64, 1), 0.0).astype(BF16)


def return_kernel(
    dom_size,
    gblocks_ref, gown_ref, gmap_ref, wup_ref,
    force_ref, fgrad_ref,
    landed, part, heard, send_sem, recv_sem,
):
    me = lax.axis_index("dom")
    quarter = lax.axis_index("edge")
    barrier = greet(dom_size)
    pl.semaphore_wait(barrier, NOFF + QUART - 1)
    copies = []
    for number in range(NOFF):
        copy = pltpu.make_async_remote_copy(
            src_ref=gblocks_ref.at[number],
            dst_ref=landed.at[number],
            send_sem=send_sem.at[number],
            recv_sem=recv_sem.at[number],
            device_id=(neighbours(dom_size, number, -1), quarter),
            device_id_type=MESH,
        )
        copy.start()
        copies.append(copy)

    low = iota((64, 128), 1) < 64
    low16 = iota((16, 128), 1) < 64
    total = jnp.zeros((GROWS, ATOMS), F32)
    for p in range(PAIRS):
        copies[2 * p].wait_recv()
        copies[2 * p + 1].wait_recv()
        even = landed[2 * p].astype(F32)
        odd = landed[2 * p + 1].astype(F32)
        top = jnp.where(low, even[0:64], pltpu.roll(odd[0:64], 64, 1))
        bottom = jnp.where(low, pltpu.roll(even[0:64], 64, 1), odd[0:64])
        pos = jnp.where(low16, even[64:80], pltpu.roll(odd[64:80], 64, 1))
        left = jnp.concatenate([top, bottom, pos], axis=0).astype(BF16)
        row = pair_rows(gmap_ref, p)
        onehot = jnp.where(iota((ATOMS, 128), 0) == row, 1.0, 0.0).astype(BF16)
        total = total + mm_nt(left, onehot)
    feat = total[0:128] + gown_ref[0:128, :]
    pos = total[128:136] + total[136:144] + gown_ref[128:136, :]
    for j in range(QUART):
        span = slice(128 * j, 128 * j + 128)
        part[j, 0:128, :] = feat[:, span]
        part[j, 128:136, :] = pos[:, span]

    sums = []
    for j in range(1, QUART):
        peer = lax.rem(quarter + j, QUART)
        copy = pltpu.make_async_remote_copy(
            src_ref=part.at[peer],
            dst_ref=heard.at[j - 1],
            send_sem=send_sem.at[NOFF + j - 1],
            recv_sem=recv_sem.at[NOFF + j - 1],
            device_id=(me, peer),
            device_id_type=MESH,
        )
        copy.start()
        sums.append(copy)
    got = part[quarter]
    for j, copy in enumerate(sums):
        copy.wait_recv()
        got = got + heard[j]
    force_ref[...] = -got[128:131]
    fgrad_ref[...] = lax.dot_general(
        got[0:128].T,
        wup_ref[...].astype(F32),
        (((1,), (1,)), ((), ())),
        precision=HIGH,
        preferred_element_type=F32,
    )
    for copy in copies + sums:
        copy.wait_send()


def on_device(
    dom_size, coordinates, features, species, ghost_map, edge_sender, edge_receiver, edge_count,
    w_up, radial_one, radial_two, radial_three, read_mix, species_out,
):
    sds = jax.ShapeDtypeStruct
    edges = QUART * EDGE_ROWS
    slots, blocks, own = pl.pallas_call(
        lambda *refs: exchange_kernel(dom_size, *refs),
        out_shape=(sds((RANKS, OWN), I32), sds((NOFF, BLK, 128), BF16), sds((CH, ATOMS), BF16)),
        in_specs=[VMEM_SPEC] * 6 + [pl.BlockSpec(memory_space=pltpu.SMEM)],
        out_specs=(VMEM_SPEC,) * 3,
        scratch_shapes=[
            pltpu.VMEM((NOFF, BLK, 128), BF16),
            pltpu.VMEM((QUART, EDGE_ROWS, 128), I32),
            pltpu.VMEM((edges, 128), F32),
            pltpu.VMEM((edges, 128), F32),
            pltpu.VMEM((edges, 128), F32),
            pltpu.VMEM((256, 384), BF16),
            pltpu.SemaphoreType.DMA((NOFF + QUART - 1,)),
            pltpu.SemaphoreType.DMA((NOFF + QUART - 1,)),
        ],
        compiler_params=pltpu.CompilerParams(
            collective_id=0, has_side_effects=True, vmem_limit_bytes=LIMIT
        ),
        name="exchange",
    )(
        features, w_up, coordinates, ghost_map,
        edge_sender.reshape(EDGE_ROWS, 128), edge_receiver.reshape(EDGE_ROWS, 128), edge_count,
    )

    edge_total = OWN * RANKS
    energy, gblocks, gown = pl.pallas_call(
        compute_kernel,
        out_shape=(sds((1, OWN), F32), sds((NOFF, BLK, 128), BF16), sds((136, ATOMS), F32)),
        in_specs=[VMEM_SPEC] * 10,
        out_specs=(VMEM_SPEC,) * 3,
        scratch_shapes=[
            pltpu.VMEM((GROUPS * GROWS, 256), BF16),
            pltpu.VMEM((256, edge_total), BF16),
            pltpu.VMEM((9 * CH, OWN), F32),
            pltpu.VMEM((3 * CH, edge_total), F32),
            pltpu.VMEM((CH, edge_total), F32),
            pltpu.VMEM((64, edge_total), F32),
            pltpu.VMEM((64, edge_total), F32),
            pltpu.VMEM((8, edge_total), F32),
            pltpu.VMEM((8, edge_total), F32),
            pltpu.VMEM((GROUPS * GROWS, 256), F32),
            pltpu.VMEM((128, 128), F32),
            pltpu.VMEM((64, 24), BF16),
            pltpu.VMEM((64, 192), BF16),
            pltpu.VMEM((384, 192), BF16),
            pltpu.VMEM((8, 192), BF16),
            pltpu.VMEM((64, 192), BF16),
            pltpu.VMEM((128, 384), BF16),
            pltpu.VMEM((24, NE), F32),
        ],
        compiler_params=pltpu.CompilerParams(vmem_limit_bytes=LIMIT),
        name="compute",
    )(
        slots, blocks, own, coordinates, species.reshape(QUART, OWN),
        radial_one, radial_two, radial_three, read_mix, species_out,
    )

    forces, feature_grad = pl.pallas_call(
        lambda *refs: return_kernel(dom_size, *refs),
        out_shape=(sds((3, OWN), F32), sds((OWN, CH), F32)),
        in_specs=[VMEM_SPEC] * 4,
        out_specs=(VMEM_SPEC,) * 2,
        scratch_shapes=[
            pltpu.VMEM((NOFF, BLK, 128), BF16),
            pltpu.VMEM((QUART, 136, 128), F32),
            pltpu.VMEM((QUART - 1, 136, 128), F32),
            pltpu.SemaphoreType.DMA((NOFF + QUART - 1,)),
            pltpu.SemaphoreType.DMA((NOFF + QUART - 1,)),
        ],
        compiler_params=pltpu.CompilerParams(
            collective_id=1, has_side_effects=True, vmem_limit_bytes=LIMIT
        ),
        name="giveback",
    )(gblocks, gown, ghost_map, w_up)
    return energy.reshape(OWN), forces, feature_grad


def solution(mesh):
    dom_size = mesh.shape["dom"]
    return jax.shard_map(
        lambda *args: on_device(dom_size, *args),
        mesh=mesh,
        in_specs=(
            P(None, "dom"),
            P("dom", None),
            P("dom"),
            P("dom", None),
            P(("dom", "edge")),
            P(("dom", "edge")),
            P("dom"),
            P(),
            P(),
            P(),
            P(),
            P(),
            P(),
        ),
        out_specs=(P(("dom", "edge")), P(None, ("dom", "edge")), P(("dom", "edge"), None)),
        check_vma=False,
    )
```

time: 1620 us -> 134 us (0.08); the launches traced: 1600 us -> 132 us
  local copies, waits for them, and re-layouts: 480 us -> 2.71 us
  other arithmetic: 447 us -> 0 us
  starting transfers between devices: 294 us -> 0 us
  waiting for transfers between devices: 254 us -> 0 us
  Pallas kernels: 0 us -> 128 us
  matrix products: 105 us -> 0 us
    gather x83 -> x0, local copies, waits for them, and re-layouts: 319 us -> none  [the longest x16 94.2 us: step_block(): jax.ops.segment_sum(message, recv_rows, num_segments=atom_count)]
    ppermute x104 -> x0, starting transfers between devices: 293 us -> none  [passed_along(): return lax.ppermute(value, axis, pairs)]
    scatter-add x68 -> x0, other arithmetic: 210 us -> none  [the longest x8 94.3 us: step_block(): jax.ops.segment_sum(message, recv_rows, num_segments=atom_count)]
    pallas_call x0 -> x3, Pallas kernels: none -> 128 us  [the longest x1 67 us: on_device(): pl.pallas_call(compute_kernel, out_shape=(sds((1, OWN), F32), sds((NOFF,...]
    ppermute x104 -> x0, waiting for transfers between devices: 120 us -> none  [passed_along(): return lax.ppermute(value, axis, pairs)]
    dot_general x77 -> x0, matrix products: 105 us -> none  [the longest x24 62.2 us: radial_part(): return jnp.dot(hidden_two, radial_three, precision=HIGH) * envelope[:, None]]
    add_any x32 -> x0, other arithmetic: 104 us -> none  [the longest x8 103 us: block_messages(): pos_send = jnp.take(positions, senders, axis=1)]
    psum x1 -> x0, waiting for transfers between devices: 101 us -> none  [on_device(): node_total = lax.psum(partial_sums, 'edge')]
  transfers between devices with their start and end apart: 107 -> 0, of which waited for: 31 -> 0; matrix products, arithmetic and copies ran while one was open for 4% -> 0% of each run, Pallas kernels for 0% -> 0%
where the time goes in v1:
time: 134 us; the launch traced here: 132 us
  Pallas kernels  128 us (96%)
  local copies, waits for them, and re-layouts  2.71 us (2%)
    pallas_call x1, Pallas kernels, on_device(): pl.pallas_call(compute_kernel, out_shape=(sds((1, OWN), F32), sds((NOFF,...  67 us
    pallas_call x1, Pallas kernels, on_device(): pl.pallas_call(lambda *refs: exchange_kernel(dom_size, *refs), out_shape=...  32.7 us
    pallas_call x1, Pallas kernels, on_device(): pl.pallas_call(lambda *refs: return_kernel(dom_size, *refs), out_shape=(s...  28.6 us
    unnamed x4, local copies, waits for them, and re-layouts  2.71 us

profile of v1, /device:TPU:3, one launch (start us, length us, event | category | flops | bytes accessed | tf_op | source)
XLA Modules:
  0.0 132.4 jit_solution(8221129810935474425)
XLA Ops:
  1.3 32.7 %exchange.1 = (s32[64,128]{1,0:T(8,128)}, bf16[26,80,128]{2,1,0:T(8,128)(2,1)}, bf16[128,512]{1,0:T(8,128)(2,1)}) custom-call(bf16[512,128]{1,0:T(8,128)(2,1)} %refs_0_.1, bf16[128,128]{1,0:T(8,128)(2,1)} %refs_3_.3, bf16[3,512]{1,0:T(4,128)(2,1)} %coord_ref.1, s32[26,64]{1,0:T(8,128)} %refs_2_.3, s32[64,128]{1,0:T(8,128)} %bitcast.4, s32[64,128]{1,0:T(8,128)} %bitcast.5, ...), custom_call_target="tpu_custom_call" | custom-call | tf_op jit(solution)/shard_map/exchange/pallas_call | solution.py:560
  34.0 67.0 %compute.1 = (f32[1,128]{1,0:T(1,128)}, bf16[26,80,128]{2,1,0:T(8,128)(2,1)}, f32[136,512]{1,0:T(8,128)}) custom-call(s32[64,128]{1,0:T(8,128)} %get-tuple-element.11.slots_ref, bf16[26,80,128]{2,1,0:T(8,128)(2,1)} %get-tuple-element.12.blocks_ref, bf16[128,512]{1,0:T(8,128)(2,1)} %get-tuple-element.13.own_ref, bf16[3,512]{1,0:T(4,128)(2,1)} %coord_ref.1, ...), custom_call_target="tpu_custom_call" | custom-call | tf_op jit(solution)/shard_map/compute/pallas_call | solution.py:585
  101.1 28.6 %giveback.1 = (f32[3,128]{1,0:T(4,128)}, f32[128,128]{1,0:T(8,128)}) custom-call(bf16[26,80,128]{2,1,0:T(8,128)(2,1)} %get-tuple-element.15.refs_0_, f32[136,512]{1,0:T(8,128)} %get-tuple-element.16.refs_1_, s32[26,64]{1,0:T(8,128)} %refs_2_.3, bf16[128,128]{1,0:T(8,128)(2,1)} %refs_3_.3), custom_call_target="tpu_custom_call" | custom-call | tf_op jit(solution)/shard_map/giveback/pallas_call | solution.py:617
  129.6 0.0 copy-start
  129.7 0.7 copy-done
  130.3 0.6 copy.19
  130.9 1.5 %copy.20 = f32[128,128]{1,0:T(8,128)} copy(f32[128,128]{1,0:T(8,128)} %get-tuple-element.24) | data formatting | bytes 131072
Async XLA Ops:
  129.6 0.7 copy-start

commit v2 on v1

--- a/solution.py
+++ b/solution.py
@@ -21,8 +21,10 @@
 EDGE_ROWS = 64
 GROUPS = 9
 GROWS = 144
-NE = 256
+PER = 16
+NE = PER * OWN
 STEPS = OWN * RANKS // NE
+SORT_ROWS = 64
 BLK = 80
 SENTINEL = 4095
 LIMIT = 56 * 1024 * 1024
@@ -76,23 +78,38 @@
     return lax.broadcasted_iota(I32, shape, dim)
 
 
-def pair_rows(gmap_ref, p):
-    return jnp.concatenate([gmap_ref[2 * p : 2 * p + 1, :], gmap_ref[2 * p + 1 : 2 * p + 2, :]], axis=1)
-
-
-def neighbours(dom_size, number, sign):
-    me = lax.axis_index("dom")
-    step = shifts(dom_size)[number] * sign
-    return lax.rem(me + (step % dom_size), dom_size)
+def fold(x):
+    parts = [x[:, 128 * j : 128 * (j + 1)] for j in range(x.shape[1] // 128)]
+    while len(parts) > 1:
+        parts = [parts[j] + parts[j + 1] for j in range(0, len(parts), 2)]
+    return parts[0]
+
+
+def map_rows(gmap_ref, core, i):
+    other = min(i + 1, PAIRS - 1)
+    return jnp.concatenate(
+        [gmap_ref[pl.ds(2 * i + core, 1), :], gmap_ref[pl.ds(2 * other + core, 1), :]], axis=1
+    )
+
+
+def offset_device(dom_size, i, core, sign):
+    me, quarter = lax.axis_index("dom"), lax.axis_index("edge")
+    even, odd = [(shifts(dom_size)[2 * i + j] * sign) % dom_size for j in (0, 1)]
+    swap_even, swap_odd = [int(OFFSETS[2 * i + j][2] != 0) for j in (0, 1)]
+    there = lax.rem(me + even + core * (odd - even), dom_size)
+    swap = swap_even + core * (swap_odd - swap_even)
+    return there, lax.rem(quarter + 2 * swap, QUART)
 
 
 def greet(dom_size):
     barrier = pltpu.get_barrier_semaphore()
     quarter = lax.axis_index("edge")
     me = lax.axis_index("dom")
-    for number in range(NOFF):
-        there = neighbours(dom_size, number, 1)
-        pl.semaphore_signal(barrier, inc=1, device_id=(there, quarter), device_id_type=MESH)
+    core = lax.rem(quarter, 2)
+    for i in range(PAIRS):
+        for sign in (1, -1):
+            there = offset_device(dom_size, i, core, sign)
+            pl.semaphore_signal(barrier, inc=1, device_id=there, device_id_type=MESH)
     for j in range(1, QUART):
         peer = lax.rem(quarter + j, QUART)
         pl.semaphore_signal(barrier, inc=1, device_id=(me, peer), device_id_type=MESH)
@@ -107,6 +124,8 @@
 ):
     me = lax.axis_index("dom")
     quarter = lax.axis_index("edge")
+    core = lax.rem(quarter, 2)
+    mate = quarter + 1 - 2 * core
     barrier = greet(dom_size)
 
     first = quarter * (EDGE_ROWS * 128)
@@ -122,6 +141,18 @@
     ).astype(BF16)
     ext = jnp.concatenate([h_t, coords], axis=0)
 
+    low = iota((64, 128), 1) < 64
+    low16 = iota((16, 128), 1) < 64
+    for i in range(0, PAIRS, 2):
+        onehot = jnp.where(iota((ATOMS, 128), 0) == map_rows(gmap_ref, core, i), 1.0, 0.0)
+        picked = mm(ext, onehot.astype(BF16))
+        top, bottom, pos = picked[0:64], picked[64:128], picked[128:144]
+        sendblk[i, 0:64, :] = jnp.where(low, top, pltpu.roll(bottom, 64, 1)).astype(BF16)
+        sendblk[i, 64:80, :] = pos.astype(BF16)
+        if i + 1 < PAIRS:
+            sendblk[i + 1, 0:64, :] = jnp.where(low, pltpu.roll(top, 64, 1), bottom).astype(BF16)
+            sendblk[i + 1, 64:80, :] = pltpu.roll(pos, 64, 1).astype(BF16)
+
     pl.semaphore_wait(barrier, NOFF + QUART - 1)
 
     copies = []
@@ -130,39 +161,26 @@
         copy = pltpu.make_async_remote_copy(
             src_ref=epack.at[quarter],
             dst_ref=epack.at[quarter],
-            send_sem=send_sem.at[NOFF + j - 1],
-            recv_sem=recv_sem.at[NOFF + j - 1],
+            send_sem=send_sem.at[PAIRS + j - 1],
+            recv_sem=recv_sem.at[PAIRS + j - 1],
             device_id=(me, peer),
             device_id_type=MESH,
         )
         copy.start()
         copies.append(copy)
 
-    low = iota((64, 128), 1) < 64
-    low16 = iota((16, 128), 1) < 64
     ghosts = []
-    for p in range(PAIRS):
-        row = pair_rows(gmap_ref, p)
-        onehot = jnp.where(iota((ATOMS, 128), 0) == row, 1.0, 0.0).astype(BF16)
-        picked = mm(ext, onehot)
-        top, bottom, pos = picked[0:64], picked[64:128], picked[128:144]
-        even = jnp.where(low, top, pltpu.roll(bottom, 64, 1))
-        odd = jnp.where(low, pltpu.roll(top, 64, 1), bottom)
-        sendblk[2 * p, 0:64, :] = even.astype(BF16)
-        sendblk[2 * p + 1, 0:64, :] = odd.astype(BF16)
-        sendblk[2 * p, 64:80, :] = jnp.where(low16, pos, 0.0).astype(BF16)
-        sendblk[2 * p + 1, 64:80, :] = jnp.where(low16, pltpu.roll(pos, 64, 1), 0.0).astype(BF16)
-        for number in (2 * p, 2 * p + 1):
-            copy = pltpu.make_async_remote_copy(
-                src_ref=sendblk.at[number],
-                dst_ref=blocks_ref.at[number],
-                send_sem=send_sem.at[number],
-                recv_sem=recv_sem.at[number],
-                device_id=(neighbours(dom_size, number, 1), quarter),
-                device_id_type=MESH,
-            )
-            copy.start()
-            ghosts.append(copy)
+    for j in range(PAIRS):
+        copy = pltpu.make_async_remote_copy(
+            src_ref=sendblk.at[j],
+            dst_ref=blocks_ref.at[core, j],
+            send_sem=send_sem.at[j],
+            recv_sem=recv_sem.at[j],
+            device_id=offset_device(dom_size, j, core, 1),
+            device_id_type=MESH,
+        )
+        copy.start()
+        ghosts.append(copy)
 
     for copy in copies:
         copy.wait_recv()
@@ -182,17 +200,17 @@
 
     def sort_step(step, carry):
         base, total = carry
-        rows = pl.ds(pl.multiple_of(step * 8, 8), 8)
+        rows = pl.ds(pl.multiple_of(step * SORT_ROWS, SORT_ROWS), SORT_ROWS)
         li8, g8, hi8 = li_s[rows, :], g_s[rows, :], hi_s[rows, :]
 
         def lane_row(x, b):
             return jnp.concatenate([x[2 * b : 2 * b + 1], x[2 * b + 1 : 2 * b + 2]], axis=1)
 
-        hots = [jnp.where(atom == lane_row(li8, b), 1.0, 0.0) for b in range(4)]
+        hots = [jnp.where(atom == lane_row(li8, b), 1.0, 0.0) for b in range(SORT_ROWS // 2)]
         hots16 = [hot.astype(BF16) for hot in hots]
         counts = mm(jnp.concatenate(hots16, axis=0), tri_s[...])
         lefts = []
-        for b in range(4):
+        for b in range(SORT_ROWS // 2):
             block = counts[OWN * b : OWN * (b + 1)]
             before = block[:, 0:256] + jnp.concatenate([base, base], axis=1)
             base = base + block[:, 256:384]
@@ -211,12 +229,23 @@
         return base, total
 
     zero = jnp.zeros((OWN, 128), F32)
-    _, total = lax.fori_loop(0, QUART * EDGE_ROWS // 8, sort_step, (zero, zero))
-    slots_ref[...] = (total[0:64] * 256.0 + total[64:128]).astype(I32)
-
+    steps = QUART * EDGE_ROWS // SORT_ROWS
+    state = lax.fori_loop(0, steps // 2, sort_step, (zero, zero))
     for copy in ghosts:
         copy.wait_recv()
-    for copy in copies + ghosts:
+    share = pltpu.make_async_remote_copy(
+        src_ref=blocks_ref.at[core],
+        dst_ref=blocks_ref.at[core],
+        send_sem=send_sem.at[PAIRS + QUART - 1],
+        recv_sem=recv_sem.at[PAIRS + QUART - 1],
+        device_id=(me, mate),
+        device_id_type=MESH,
+    )
+    share.start()
+    _, total = lax.fori_loop(steps // 2, steps, sort_step, state)
+    slots_ref[...] = (total[0:64] * 256.0 + total[64:128]).astype(I32)
+    share.wait_recv()
+    for copy in copies + ghosts + [share]:
         copy.wait_send()
 
 
@@ -242,8 +271,8 @@
     tab[GROWS * 8 : GROWS * 9, :] = jnp.zeros((GROWS, 256), BF16)
     for p in range(PAIRS):
         g, at = 2 + p // 2, 128 * (p % 2)
-        even = blocks_ref[2 * p].astype(F32)
-        odd = blocks_ref[2 * p + 1].astype(F32)
+        even = blocks_ref[0, p].astype(F32)
+        odd = blocks_ref[1, p].astype(F32)
         top = jnp.where(low, even[0:64], pltpu.roll(odd[0:64], 64, 1))
         bottom = jnp.where(low, pltpu.roll(even[0:64], 64, 1), odd[0:64])
         pos = jnp.where(low16, even[64:80], pltpu.roll(odd[64:80], 64, 1))
@@ -272,7 +301,7 @@
     my_coords = coord_ref[:, mine].astype(F32)
     for c in range(3):
         mc = jnp.broadcast_to(my_coords[c : c + 1], (8, 128))
-        myc[8 * c : 8 * c + 8, :] = jnp.concatenate([mc, mc], axis=1)
+        myc[8 * c : 8 * c + 8, :] = jnp.concatenate([mc] * PER, axis=1)
 
     beta = jnp.zeros((8, NE), F32)
     for n in range(8):
@@ -280,7 +309,7 @@
 
     def slot_row(step):
         s = jnp.concatenate(
-            [slots_ref[pl.ds(2 * step, 1), :], slots_ref[pl.ds(2 * step + 1, 1), :]], axis=1
+            [slots_ref[pl.ds(PER * step + j, 1), :] for j in range(PER)], axis=1
         )
         return jnp.broadcast_to(s, (8, NE))
 
@@ -346,7 +375,7 @@
             for m in range(9):
                 msg = ds[degree[m]] if m == 0 else ds[degree[m]] * ys[m]
                 at = 128 * m + 8 * t
-                acc[at : at + 8, :] += msg[:, 0:128] + msg[:, 128:256]
+                acc[at : at + 8, :] += fold(msg)
         return carry
 
     lax.fori_loop(0, STEPS, fwd, 0)
@@ -400,7 +429,7 @@
             da = []
             for m in range(9):
                 v = acc[128 * m + 8 * t : 128 * m + 8 * t + 8, :]
-                da.append(jnp.concatenate([v, v], axis=1))
+                da.append(jnp.concatenate([v] * PER, axis=1))
             t0 = da[0]
             t1 = x * da[1] + y * da[2] + z * da[3]
             t2 = ys[4] * da[4]
@@ -448,7 +477,7 @@
             mask = jnp.where(group16 == k, 1.0, 0.0).astype(BF16)
             lefts.extend(flow[16 * t : 16 * t + 16] * mask for t in range(9))
         scat[...] += mm_nt(jnp.concatenate(lefts, axis=0), hot_s[:, lanes])
-        return down + drel[:, 0:128] + drel[:, 128:256]
+        return down + fold(drel)
 
     down = lax.fori_loop(0, STEPS, bwd, jnp.zeros((8, 128), F32))
 
@@ -471,30 +500,48 @@
         pos = jnp.concatenate([pos_hi, pos - pos_hi], axis=0)
         even = jnp.where(low, top, pltpu.roll(bottom, 64, 1))
         odd = jnp.where(low, pltpu.roll(top, 64, 1), bottom)
-        gblocks_ref[2 * p, 0:64, :] = even.astype(BF16)
-        gblocks_ref[2 * p + 1, 0:64, :] = odd.astype(BF16)
-        gblocks_ref[2 * p, 64:80, :] = jnp.where(low16, pos, 0.0).astype(BF16)
-        gblocks_ref[2 * p + 1, 64:80, :] = jnp.where(low16, pltpu.roll(pos, 64, 1), 0.0).astype(BF16)
+        gblocks_ref[0, p, 0:64, :] = even.astype(BF16)
+        gblocks_ref[1, p, 0:64, :] = odd.astype(BF16)
+        gblocks_ref[0, p, 64:80, :] = jnp.where(low16, pos, 0.0).astype(BF16)
+        gblocks_ref[1, p, 64:80, :] = jnp.where(low16, pltpu.roll(pos, 64, 1), 0.0).astype(BF16)
+
+
+def landed_block(copies, landed, i):
+    copies[i].wait_recv()
+    return landed[i].astype(F32)
 
 
 def return_kernel(
     dom_size,
     gblocks_ref, gown_ref, gmap_ref, wup_ref,
     force_ref, fgrad_ref,
-    landed, part, heard, send_sem, recv_sem,
+    matebuf, sendblk, landed, part, heard, send_sem, recv_sem,
 ):
     me = lax.axis_index("dom")
     quarter = lax.axis_index("edge")
+    core = lax.rem(quarter, 2)
+    mate = quarter + 1 - 2 * core
     barrier = greet(dom_size)
     pl.semaphore_wait(barrier, NOFF + QUART - 1)
+    share = pltpu.make_async_remote_copy(
+        src_ref=gblocks_ref.at[1 - core],
+        dst_ref=matebuf,
+        send_sem=send_sem.at[PAIRS + QUART - 1],
+        recv_sem=recv_sem.at[PAIRS + QUART - 1],
+        device_id=(me, mate),
+        device_id_type=MESH,
+    )
+    share.start()
+    share.wait_recv()
     copies = []
-    for number in range(NOFF):
+    for i in range(PAIRS):
+        sendblk[i] = (gblocks_ref[core, i].astype(F32) + matebuf[i].astype(F32)).astype(BF16)
         copy = pltpu.make_async_remote_copy(
-            src_ref=gblocks_ref.at[number],
-            dst_ref=landed.at[number],
-            send_sem=send_sem.at[number],
-            recv_sem=recv_sem.at[number],
-            device_id=(neighbours(dom_size, number, -1), quarter),
+            src_ref=sendblk.at[i],
+            dst_ref=landed.at[i],
+            send_sem=send_sem.at[i],
+            recv_sem=recv_sem.at[i],
+            device_id=offset_device(dom_size, i, core, -1),
             device_id_type=MESH,
         )
         copy.start()
@@ -503,18 +550,15 @@
     low = iota((64, 128), 1) < 64
     low16 = iota((16, 128), 1) < 64
     total = jnp.zeros((GROWS, ATOMS), F32)
-    for p in range(PAIRS):
-        copies[2 * p].wait_recv()
-        copies[2 * p + 1].wait_recv()
-        even = landed[2 * p].astype(F32)
-        odd = landed[2 * p + 1].astype(F32)
+    for i in range(0, PAIRS, 2):
+        even = landed_block(copies, landed, i)
+        odd = landed_block(copies, landed, i + 1) if i + 1 < PAIRS else jnp.zeros((BLK, 128), F32)
         top = jnp.where(low, even[0:64], pltpu.roll(odd[0:64], 64, 1))
         bottom = jnp.where(low, pltpu.roll(even[0:64], 64, 1), odd[0:64])
         pos = jnp.where(low16, even[64:80], pltpu.roll(odd[64:80], 64, 1))
         left = jnp.concatenate([top, bottom, pos], axis=0).astype(BF16)
-        row = pair_rows(gmap_ref, p)
-        onehot = jnp.where(iota((ATOMS, 128), 0) == row, 1.0, 0.0).astype(BF16)
-        total = total + mm_nt(left, onehot)
+        onehot = jnp.where(iota((ATOMS, 128), 0) == map_rows(gmap_ref, core, i), 1.0, 0.0)
+        total = total + mm_nt(left, onehot.astype(BF16))
     feat = total[0:128] + gown_ref[0:128, :]
     pos = total[128:136] + total[136:144] + gown_ref[128:136, :]
     for j in range(QUART):
@@ -528,8 +572,8 @@
         copy = pltpu.make_async_remote_copy(
             src_ref=part.at[peer],
             dst_ref=heard.at[j - 1],
-            send_sem=send_sem.at[NOFF + j - 1],
-            recv_sem=recv_sem.at[NOFF + j - 1],
+            send_sem=send_sem.at[PAIRS + j - 1],
+            recv_sem=recv_sem.at[PAIRS + j - 1],
             device_id=(me, peer),
             device_id_type=MESH,
         )
@@ -547,44 +591,16 @@
         precision=HIGH,
         preferred_element_type=F32,
     )
-    for copy in copies + sums:
+    for copy in copies + sums + [share]:
         copy.wait_send()
 
 
-def on_device(
-    dom_size, coordinates, features, species, ghost_map, edge_sender, edge_receiver, edge_count,
-    w_up, radial_one, radial_two, radial_three, read_mix, species_out,
-):
+def compute_call(*operands):
     sds = jax.ShapeDtypeStruct
-    edges = QUART * EDGE_ROWS
-    slots, blocks, own = pl.pallas_call(
-        lambda *refs: exchange_kernel(dom_size, *refs),
-        out_shape=(sds((RANKS, OWN), I32), sds((NOFF, BLK, 128), BF16), sds((CH, ATOMS), BF16)),
-        in_specs=[VMEM_SPEC] * 6 + [pl.BlockSpec(memory_space=pltpu.SMEM)],
-        out_specs=(VMEM_SPEC,) * 3,
-        scratch_shapes=[
-            pltpu.VMEM((NOFF, BLK, 128), BF16),
-            pltpu.VMEM((QUART, EDGE_ROWS, 128), I32),
-            pltpu.VMEM((edges, 128), F32),
-            pltpu.VMEM((edges, 128), F32),
-            pltpu.VMEM((edges, 128), F32),
-            pltpu.VMEM((256, 384), BF16),
-            pltpu.SemaphoreType.DMA((NOFF + QUART - 1,)),
-            pltpu.SemaphoreType.DMA((NOFF + QUART - 1,)),
-        ],
-        compiler_params=pltpu.CompilerParams(
-            collective_id=0, has_side_effects=True, vmem_limit_bytes=LIMIT
-        ),
-        name="exchange",
-    )(
-        features, w_up, coordinates, ghost_map,
-        edge_sender.reshape(EDGE_ROWS, 128), edge_receiver.reshape(EDGE_ROWS, 128), edge_count,
-    )
-
     edge_total = OWN * RANKS
-    energy, gblocks, gown = pl.pallas_call(
+    return pl.pallas_call(
         compute_kernel,
-        out_shape=(sds((1, OWN), F32), sds((NOFF, BLK, 128), BF16), sds((136, ATOMS), F32)),
+        out_shape=(sds((1, OWN), F32), sds((2, PAIRS, BLK, 128), BF16), sds((136, ATOMS), F32)),
         in_specs=[VMEM_SPEC] * 10,
         out_specs=(VMEM_SPEC,) * 3,
         scratch_shapes=[
@@ -609,28 +625,70 @@
         ],
         compiler_params=pltpu.CompilerParams(vmem_limit_bytes=LIMIT),
         name="compute",
-    )(
-        slots, blocks, own, coordinates, species.reshape(QUART, OWN),
-        radial_one, radial_two, radial_three, read_mix, species_out,
-    )
-
-    forces, feature_grad = pl.pallas_call(
+    )(*operands)
+
+
+def exchange_call(dom_size, *operands):
+    sds = jax.ShapeDtypeStruct
+    edges = QUART * EDGE_ROWS
+    return pl.pallas_call(
+        lambda *refs: exchange_kernel(dom_size, *refs),
+        out_shape=(sds((RANKS, OWN), I32), sds((2, PAIRS, BLK, 128), BF16), sds((CH, ATOMS), BF16)),
+        in_specs=[VMEM_SPEC] * 6 + [pl.BlockSpec(memory_space=pltpu.SMEM)],
+        out_specs=(VMEM_SPEC,) * 3,
+        scratch_shapes=[
+            pltpu.VMEM((PAIRS, BLK, 128), BF16),
+            pltpu.VMEM((QUART, EDGE_ROWS, 128), I32),
+            pltpu.VMEM((edges, 128), F32),
+            pltpu.VMEM((edges, 128), F32),
+            pltpu.VMEM((edges, 128), F32),
+            pltpu.VMEM((256, 384), BF16),
+            pltpu.SemaphoreType.DMA((PAIRS + QUART,)),
+            pltpu.SemaphoreType.DMA((PAIRS + QUART,)),
+        ],
+        compiler_params=pltpu.CompilerParams(
+            collective_id=0, has_side_effects=True, vmem_limit_bytes=LIMIT
+        ),
+        name="exchange",
+    )(*operands)
+
+
+def giveback_call(dom_size, *operands):
+    sds = jax.ShapeDtypeStruct
+    return pl.pallas_call(
         lambda *refs: return_kernel(dom_size, *refs),
         out_shape=(sds((3, OWN), F32), sds((OWN, CH), F32)),
         in_specs=[VMEM_SPEC] * 4,
         out_specs=(VMEM_SPEC,) * 2,
         scratch_shapes=[
-            pltpu.VMEM((NOFF, BLK, 128), BF16),
+            pltpu.VMEM((PAIRS, BLK, 128), BF16),
+            pltpu.VMEM((PAIRS, BLK, 128), BF16),
+            pltpu.VMEM((PAIRS, BLK, 128), BF16),
             pltpu.VMEM((QUART, 136, 128), F32),
             pltpu.VMEM((QUART - 1, 136, 128), F32),
-            pltpu.SemaphoreType.DMA((NOFF + QUART - 1,)),
-            pltpu.SemaphoreType.DMA((NOFF + QUART - 1,)),
+            pltpu.SemaphoreType.DMA((PAIRS + QUART,)),
+            pltpu.SemaphoreType.DMA((PAIRS + QUART,)),
         ],
         compiler_params=pltpu.CompilerParams(
             collective_id=1, has_side_effects=True, vmem_limit_bytes=LIMIT
         ),
         name="giveback",
-    )(gblocks, gown, ghost_map, w_up)
+    )(*operands)
+
+
+def on_device(
+    dom_size, coordinates, features, species, ghost_map, edge_sender, edge_receiver, edge_count,
+    w_up, radial_one, radial_two, radial_three, read_mix, species_out,
+):
+    slots, blocks, own = exchange_call(
+        dom_size, features, w_up, coordinates, ghost_map,
+        edge_sender.reshape(EDGE_ROWS, 128), edge_receiver.reshape(EDGE_ROWS, 128), edge_count,
+    )
+    energy, gblocks, gown = compute_call(
+        slots, blocks, own, coordinates, species.reshape(QUART, OWN),
+        radial_one, radial_two, radial_three, read_mix, species_out,
+    )
+    forces, feature_grad = giveback_call(dom_size, gblocks, gown, ghost_map, w_up)
     return energy.reshape(OWN), forces, feature_grad
 
 

time: 134 us -> 86.2 us (0.64)
  Pallas kernels: 128 us -> 81.8 us
    pallas_call x3, Pallas kernels: 128 us -> 81.8 us  [the longest x1 33.4 us: compute_call(): pl.pallas_call(compute_kernel, out_shape=(sds((1, OWN), F32), sds((2, PAI...]
where the time goes in v2:
time: 86.2 us; the launch traced here: 85.8 us
  Pallas kernels  81.8 us (95%)
  local copies, waits for them, and re-layouts  2.71 us (3%)
  between operations  1.3 us (2%)
    pallas_call x1, Pallas kernels, compute_call(): pl.pallas_call(compute_kernel, out_shape=(sds((1, OWN), F32), sds((2, PAI...  33.4 us
    pallas_call x1, Pallas kernels, exchange_call(): pl.pallas_call(lambda *refs: exchange_kernel(dom_size, *refs), out_shape=...  24.2 us
    pallas_call x1, Pallas kernels, giveback_call(): pl.pallas_call(lambda *refs: return_kernel(dom_size, *refs), out_shape=(s...  24.2 us
    unnamed x4, local copies, waits for them, and re-layouts  2.71 us

profile of v2, /device:TPU:3, one launch (start us, length us, event | category | flops | bytes accessed | tf_op | source)
XLA Modules:
  0.0 85.8 jit_solution(12631632331758838817)
XLA Ops:
  1.3 24.2 %exchange.1 = (s32[64,128]{1,0:T(8,128)}, bf16[2,13,80,128]{3,2,1,0:T(8,128)(2,1)}, bf16[128,512]{1,0:T(8,128)(2,1)}) custom-call(bf16[512,128]{1,0:T(8,128)(2,1)} %refs_0_.1, bf16[128,128]{1,0:T(8,128)(2,1)} %refs_3_.3, bf16[3,512]{1,0:T(4,128)(2,1)} %coord_ref.1, s32[26,64]{1,0:T(8,128)} %refs_2_.3, s32[64,128]{1,0:T(8,128)} %bitcast.4, ...), custom_call_target="tpu_custom_call" | custom-call | tf_op jit(solution)/shard_map/exchange/pallas_call | solution.py:634
  25.5 33.4 %compute.1 = (f32[1,128]{1,0:T(1,128)}, bf16[2,13,80,128]{3,2,1,0:T(8,128)(2,1)}, f32[136,512]{1,0:T(8,128)}) custom-call(s32[64,128]{1,0:T(8,128)} %get-tuple-element.11.slots_ref, bf16[2,13,80,128]{3,2,1,0:T(8,128)(2,1)} %get-tuple-element.12.blocks_ref, bf16[128,512]{1,0:T(8,128)(2,1)} %get-tuple-element.13.own_ref, bf16[3,512]{1,0:T(4,128)(2,1)} %coord_ref.1, ...), custom_call_target="tpu_custom_call" | custom-call | tf_op jit(solution)/shard_map/compute/pallas_call | solution.py:601
  58.9 24.2 %giveback.1 = (f32[3,128]{1,0:T(4,128)}, f32[128,128]{1,0:T(8,128)}) custom-call(bf16[2,13,80,128]{3,2,1,0:T(8,128)(2,1)} %get-tuple-element.15.refs_0_, f32[136,512]{1,0:T(8,128)} %get-tuple-element.16.refs_1_, s32[26,64]{1,0:T(8,128)} %refs_2_.3, bf16[128,128]{1,0:T(8,128)(2,1)} %refs_3_.3), custom_call_target="tpu_custom_call" | custom-call | tf_op jit(solution)/shard_map/giveback/pallas_call | solution.py:658
  83.1 0.0 copy-start
  83.1 0.7 copy-done
  83.7 0.6 copy.19
  84.3 1.5 %copy.20 = f32[128,128]{1,0:T(8,128)} copy(f32[128,128]{1,0:T(8,128)} %get-tuple-element.24) | data formatting | bytes 131072
Async XLA Ops:
  83.1 0.7 copy-start

commit v3 on v2

--- a/solution.py
+++ b/solution.py
@@ -21,6 +21,7 @@
 EDGE_ROWS = 64
 GROUPS = 9
 GROWS = 144
+TROWS = 1232
 PER = 16
 NE = PER * OWN
 STEPS = OWN * RANKS // NE
@@ -116,11 +117,21 @@
     return barrier
 
 
-def exchange_kernel(
+def landed_block(copies, landed, i):
+    copies[i].wait_recv()
+    return landed[i].astype(F32)
+
+
+def interaction_kernel(
     dom_size,
-    feat_ref, wup_ref, coord_ref, gmap_ref, snd_ref, rcv_ref, cnt_ref,
-    slots_ref, blocks_ref, own_ref,
-    sendblk, epack, li_s, g_s, hi_s, tri_s, send_sem, recv_sem,
+    feat_ref, wup_ref, coord_ref, gmap_ref, snd_ref, rcv_ref, cnt_ref, species_ref,
+    w1_ref, w2_ref, w3_ref, mix_ref, sp_ref,
+    energy_ref, grad_ref,
+    slots_ref, blocks_ref, own_ref, gblocks_ref, gown_ref,
+    sendblk, epack, li_s, g_s, hi_s, tri_s,
+    tab, tab32, dh_s, hot_s, acc, rad_s, h_s, d1_s, d2_s, bas_s, row_s, scat, sp_s,
+    w1f, w2f, w3f, w1b, w2b, w3b, myc,
+    matebuf, backblk, landed, part, heard, send_sem, recv_sem, back_send_sem, back_recv_sem,
 ):
     me = lax.axis_index("dom")
     quarter = lax.axis_index("edge")
@@ -143,6 +154,8 @@
 
     low = iota((64, 128), 1) < 64
     low16 = iota((16, 128), 1) < 64
+    low8 = iota((8, 128), 1) < 64
+    sub8 = iota((8, 128), 0)
     for i in range(0, PAIRS, 2):
         onehot = jnp.where(iota((ATOMS, 128), 0) == map_rows(gmap_ref, core, i), 1.0, 0.0)
         picked = mm(ext, onehot.astype(BF16))
@@ -181,6 +194,40 @@
         )
         copy.start()
         ghosts.append(copy)
+
+    coords = coord_ref[...].astype(F32)
+    coords8 = jnp.concatenate([coords, jnp.zeros((5, ATOMS), F32)], axis=0)
+    def place(g, lanes, rows):
+        for t in range(17):
+            tab32[8 * (GROUPS * t + g) : 8 * (GROUPS * t + g) + 8, lanes] = rows[8 * t : 8 * t + 8]
+
+    for g in range(2):
+        span = slice(256 * g, 256 * g + 256)
+        place(g, slice(0, 256), jnp.concatenate([own_ref[:, span].astype(F32), coords8[:, span]], axis=0))
+    place(8, slice(0, 256), jnp.zeros((136, 256), F32))
+    tab32[8 * GROUPS * 17 :, :] = jnp.zeros((TROWS - 8 * GROUPS * 17, 256), F32)
+    w1f[...] = weight_stack(w1_ref[...].T)
+    w2f[...] = weight_stack(w2_ref[...].T)
+    w3f[...] = weight_stack(w3_ref[...].T)
+    w1b[...] = weight_stack(w1_ref[...])
+    w2b[...] = weight_stack(w2_ref[...])
+    hi, lo = split(w3_ref[...])
+    w3b[...] = jnp.concatenate([hi, lo], axis=0)
+
+    acc[...] = jnp.zeros(acc.shape, F32)
+    scat[...] = jnp.zeros(scat.shape, F32)
+    mine = pl.ds(pl.multiple_of(quarter * OWN, OWN), OWN)
+    my_coords = coord_ref[:, mine].astype(F32)
+    for c in range(3):
+        mc = jnp.broadcast_to(my_coords[c : c + 1], (8, 128))
+        myc[8 * c : 8 * c + 8, :] = jnp.concatenate([mc] * PER, axis=1)
+
+    beta = jnp.zeros((8, NE), F32)
+    for n in range(8):
+        beta = jnp.where(iota((8, NE), 0) == n, 0.4 * 15.0 ** (n / 7.0), beta)
+
+    sp_s[...] = jnp.zeros((128, 128), F32)
+    sp_s[0:89, :] = sp_ref[...]
 
     for copy in copies:
         copy.wait_recv()
@@ -249,63 +296,19 @@
         copy.wait_send()
 
 
-def compute_kernel(
-    slots_ref, blocks_ref, own_ref, coord_ref, species_ref,
-    w1_ref, w2_ref, w3_ref, mix_ref, sp_ref,
-    energy_ref, gblocks_ref, gown_ref,
-    tab, hot_s, acc, rad_s, h_s, d1_s, d2_s, bas_s, row_s, scat, sp_s,
-    w1f, w2f, w3f, w1b, w2b, w3b, myc,
-):
-    quarter = lax.axis_index("edge")
-    lane = iota((64, 128), 1)
-    low = lane < 64
-    low8 = iota((8, 128), 1) < 64
-    low16 = iota((16, 128), 1) < 64
-    sub8 = iota((8, 128), 0)
-
-    coords = coord_ref[...].astype(F32)
-    coords16 = jnp.concatenate([coords, jnp.zeros((13, ATOMS), F32)], axis=0).astype(BF16)
-    for g in range(2):
-        tab[GROWS * g : GROWS * g + 128, :] = own_ref[:, 256 * g : 256 * g + 256]
-        tab[GROWS * g + 128 : GROWS * (g + 1), :] = coords16[:, 256 * g : 256 * g + 256]
-    tab[GROWS * 8 : GROWS * 9, :] = jnp.zeros((GROWS, 256), BF16)
     for p in range(PAIRS):
         g, at = 2 + p // 2, 128 * (p % 2)
         even = blocks_ref[0, p].astype(F32)
         odd = blocks_ref[1, p].astype(F32)
         top = jnp.where(low, even[0:64], pltpu.roll(odd[0:64], 64, 1))
         bottom = jnp.where(low, pltpu.roll(even[0:64], 64, 1), odd[0:64])
-        pos = jnp.where(low16, even[64:80], pltpu.roll(odd[64:80], 64, 1))
+        pos = jnp.where(low8, even[64:72], pltpu.roll(odd[64:72], 64, 1))
         oe, oo = OFFSETS[2 * p], OFFSETS[2 * p + 1]
-        off = jnp.zeros((16, 128), F32)
-        sub16 = iota((16, 128), 0)
         for c in range(3):
             if oe[c] != 0 or oo[c] != 0:
-                off = jnp.where(sub16 == 3 + c, jnp.where(low16, float(oe[c]), float(oo[c])), off)
-        pos = pos + off
-        tab[GROWS * g : GROWS * g + 64, at : at + 128] = top.astype(BF16)
-        tab[GROWS * g + 64 : GROWS * g + 128, at : at + 128] = bottom.astype(BF16)
-        tab[GROWS * g + 128 : GROWS * (g + 1), at : at + 128] = pos.astype(BF16)
-
-    w1f[...] = weight_stack(w1_ref[...].T)
-    w2f[...] = weight_stack(w2_ref[...].T)
-    w3f[...] = weight_stack(w3_ref[...].T)
-    w1b[...] = weight_stack(w1_ref[...])
-    w2b[...] = weight_stack(w2_ref[...])
-    hi, lo = split(w3_ref[...])
-    w3b[...] = jnp.concatenate([hi, lo], axis=0)
-
-    acc[...] = jnp.zeros(acc.shape, F32)
-    scat[...] = jnp.zeros(scat.shape, F32)
-    mine = pl.ds(pl.multiple_of(quarter * OWN, OWN), OWN)
-    my_coords = coord_ref[:, mine].astype(F32)
-    for c in range(3):
-        mc = jnp.broadcast_to(my_coords[c : c + 1], (8, 128))
-        myc[8 * c : 8 * c + 8, :] = jnp.concatenate([mc] * PER, axis=1)
-
-    beta = jnp.zeros((8, NE), F32)
-    for n in range(8):
-        beta = jnp.where(iota((8, NE), 0) == n, 0.4 * 15.0 ** (n / 7.0), beta)
+                pos = jnp.where(sub8 == 3 + c, jnp.where(low8, float(oe[c]), float(oo[c])), pos)
+        place(g, slice(at, at + 128), jnp.concatenate([top, bottom, pos], axis=0))
+    tab[...] = tab32[...].astype(BF16)
 
     def slot_row(step):
         s = jnp.concatenate(
@@ -319,8 +322,12 @@
 
     degree = [0, 1, 1, 1, 2, 2, 2, 2, 2]
 
-    def fwd(step, carry):
-        lanes = pl.ds(pl.multiple_of(step * NE, NE), NE)
+    def act(pre):
+        sig = 0.5 + 0.5 * jnp.tanh(0.5 * pre)
+        out = pre * sig
+        return out, sig + out * (1.0 - sig)
+
+    def gather(step, lanes, _):
         s = slot_row(step)
         group = s >> 8
         hi = s & 255
@@ -332,14 +339,18 @@
         hot_s[:, lanes] = onehot
         got = mm(tab[...], onehot)
         masks = [group == k for k in range(GROUPS)]
-        rows = []
         for t in range(17):
             v = jnp.zeros((8, NE), F32)
             for k in range(GROUPS):
-                at = GROWS * k + 8 * t
+                at = 8 * (GROUPS * t + k)
                 v = jnp.where(masks[k], got[at : at + 8], v)
-            rows.append(v)
-        pos = rows[16]
+            if t < 16:
+                h_s[8 * t : 8 * t + 8, lanes] = v
+        return v, valid
+
+    def radial_one(step, lanes, given):
+        pos, valid = given
+        sub = iota((8, NE), 0)
         rel = []
         for c in range(3):
             sent = pos[c : c + 1] - pos[3 + c : 4 + c]
@@ -347,35 +358,48 @@
         x, y, z = rel
         dsq = x * x + y * y + z * z
         e0 = jnp.maximum(0.0, 1.0 - dsq * 0.25) * valid
-        env = e0 * e0
         basis = jnp.exp(-dsq * beta)
         packed = jnp.zeros((8, NE), F32)
-        for j, v in enumerate((x, y, z, dsq, env, e0)):
+        for j, v in enumerate((x, y, z, dsq, e0 * e0, e0)):
             packed = jnp.where(sub == j, v, packed)
         row_s[:, lanes] = packed
         bas_s[:, lanes] = basis
-
-        def act(pre):
-            sig = 0.5 + 0.5 * jnp.tanh(0.5 * pre)
-            out = pre * sig
-            return out, sig + out * (1.0 - sig)
-
-        h1, d1 = act(mm(w1f[...], value_stack(basis)))
+        return mm(w1f[...], value_stack(basis))
+
+    def radial_two(step, lanes, pre):
+        h1, d1 = act(pre)
         d1_s[:, lanes] = d1
-        h2, d2 = act(mm(w2f[...], value_stack(h1)))
+        return mm(w2f[...], value_stack(h1))
+
+    def radial_three(step, lanes, pre):
+        h2, d2 = act(pre)
         d2_s[:, lanes] = d2
-        rad = mm(w3f[...], value_stack(h2))
-        rad_s[:, lanes] = rad
+        rad_s[:, lanes] = mm(w3f[...], value_stack(h2))
+
+    def row_values(lanes):
+        rows = row_s[:, lanes]
+        return [jnp.broadcast_to(rows[j : j + 1], (8, NE)) for j in range(6)]
+
+    def gather_sums(step, lanes, _):
+        x, y, z, dsq, env, _ = row_values(lanes)
         ys = harmonic(x, y, z, dsq)
         for t in range(16):
-            h = rows[t]
-            h_s[8 * t : 8 * t + 8, lanes] = h
-            he = h * env
-            ds = [he * rad[128 * l + 8 * t : 128 * l + 8 * t + 8] for l in range(3)]
+            he = h_s[8 * t : 8 * t + 8, lanes] * env
+            ds = [he * rad_s[128 * l + 8 * t : 128 * l + 8 * t + 8, lanes] for l in range(3)]
             for m in range(9):
                 msg = ds[degree[m]] if m == 0 else ds[degree[m]] * ys[m]
                 at = 128 * m + 8 * t
                 acc[at : at + 8, :] += fold(msg)
+
+    def staged(stages, step):
+        lanes = pl.ds(pl.multiple_of(step * NE, NE), NE)
+        held = None
+        for stage in stages:
+            held = stage(step, lanes, held)
+        return held
+
+    def fwd(step, carry):
+        staged([gather, radial_one, radial_two, radial_three, gather_sums], step)
         return carry
 
     lax.fori_loop(0, STEPS, fwd, 0)
@@ -395,8 +419,6 @@
     pre = mm_high(mix_ref[...].T, inv)
     sig = 0.5 + 0.5 * jnp.tanh(0.5 * pre)
     hid = pre * sig
-    sp_s[...] = jnp.zeros((128, 128), F32)
-    sp_s[0:89, :] = sp_ref[...]
     kinds = species_ref[pl.ds(quarter, 1), :]
     kind_hot = jnp.where(iota((128, 128), 0) == kinds, 1.0, 0.0)
     per_kind = mm_high(sp_s[...].T, kind_hot)
@@ -416,11 +438,8 @@
     acc[896:1024, :] = 2.0 * g2 * (xx - zz) + g4 * (vx * vx - vz * vz)
     acc[1024:1152, :] = 2.0 * g2 * (yy - zz) + g4 * (vy * vy - vz * vz)
 
-    def bwd(step, down):
-        lanes = pl.ds(pl.multiple_of(step * NE, NE), NE)
-        group = slot_row(step) >> 8
-        rows = row_s[:, lanes]
-        x, y, z, dsq, env, e0 = [jnp.broadcast_to(rows[j : j + 1], (8, NE)) for j in range(6)]
+    def edge_grads(step, lanes, _):
+        x, y, z, dsq, env, _ = row_values(lanes)
         ys = harmonic(x, y, z, dsq)
         denv = jnp.zeros((8, NE), F32)
         dys = [jnp.zeros((8, NE), F32) for _ in range(9)]
@@ -447,15 +466,27 @@
             d1, d2 = he * rs[1], he * rs[2]
             for m in range(1, 9):
                 dys[m] = dys[m] + (d1 if m < 4 else d2) * da[m]
+        drad = jnp.concatenate(drs[0] + drs[1] + drs[2], axis=0).astype(BF16)
+        both = mm(w3b[...], drad)
+        dh_s[0:128, lanes] = jnp.concatenate(dhs, axis=0).astype(BF16)
+        return denv, dys, both
+
+    def radial_back_two(step, lanes, given):
+        denv, dys, both = given
+        dp2 = (both[0:64] + both[64:128]) * d2_s[:, lanes]
+        return denv, dys, mm(w2b[...], value_stack(dp2))
+
+    def radial_back_one(step, lanes, given):
+        denv, dys, dh1 = given
+        return denv, dys, mm(w1b[...], value_stack(dh1 * d1_s[:, lanes]))
+
+    def position_grads(step, lanes, given):
+        denv, dys, dbas = given
 
         def total(v):
             return jnp.broadcast_to(jnp.sum(v, axis=0, keepdims=True), (8, NE))
 
-        drad = jnp.concatenate(drs[0] + drs[1] + drs[2], axis=0).astype(BF16)
-        both = mm(w3b[...], drad)
-        dp2 = (both[0:64] + both[64:128]) * d2_s[:, lanes]
-        dp1 = mm(w2b[...], value_stack(dp2)) * d1_s[:, lanes]
-        dbas = mm(w1b[...], value_stack(dp1))
+        x, y, z, _, _, e0 = row_values(lanes)
         denv = total(denv)
         dys = [None] + [total(v) for v in dys[1:]]
         ddsq = (
@@ -468,26 +499,29 @@
         dy = dys[2] + x * dys[4] + z * dys[5] + 2.0 * y * dys[8] + y * two
         dz = dys[3] + y * dys[5] + x * dys[6] + z * two
         sub = iota((8, NE), 0)
-        drel = jnp.where(sub == 0, dx, jnp.where(sub == 1, dy, jnp.where(sub == 2, dz, 0.0)))
-        drel_hi = drel.astype(BF16).astype(F32)
-        flow = jnp.concatenate(dhs + [drel_hi, drel - drel_hi], axis=0).astype(BF16)
+        return jnp.where(sub == 0, dx, jnp.where(sub == 1, dy, jnp.where(sub == 2, dz, 0.0)))
+
+    def masked(step, lanes, groups):
+        group = slot_row(step) >> 8
         group16 = jnp.concatenate([group, group], axis=0)
         lefts = []
-        for k in range(GROUPS):
+        for k in groups:
             mask = jnp.where(group16 == k, 1.0, 0.0).astype(BF16)
-            lefts.extend(flow[16 * t : 16 * t + 16] * mask for t in range(9))
-        scat[...] += mm_nt(jnp.concatenate(lefts, axis=0), hot_s[:, lanes])
-        return down + fold(drel)
+            lefts.extend(dh_s[16 * t : 16 * t + 16, lanes] * mask for t in range(GROWS // 16))
+        return jnp.concatenate(lefts, axis=0)
+
+    def spread(step, lanes, drel):
+        drel_hi = drel.astype(BF16).astype(F32)
+        dh_s[128:144, lanes] = jnp.concatenate([drel_hi, drel - drel_hi], axis=0).astype(BF16)
+        scat[2 * GROWS :, :] += mm_nt(masked(step, lanes, range(2, GROUPS)), hot_s[:, lanes])
+        return fold(drel)
+
+    def bwd(step, down):
+        stages = [edge_grads, radial_back_two, radial_back_one, position_grads, spread]
+        return down + staged(stages, step)
 
     down = lax.fori_loop(0, STEPS, bwd, jnp.zeros((8, 128), F32))
 
-    for g in range(2):
-        span = slice(256 * g, 256 * g + 256)
-        gown_ref[0:128, span] = scat[GROWS * g : GROWS * g + 128, :]
-        gown_ref[128:136, span] = (
-            scat[GROWS * g + 128 : GROWS * g + 136, :] + scat[GROWS * g + 136 : GROWS * g + 144, :]
-        )
-    gown_ref[128:136, mine] = gown_ref[128:136, mine] - down
     for p in range(PAIRS):
         g, at = 2 + p // 2, 128 * (p % 2)
         top = scat[GROWS * g : GROWS * g + 64, at : at + 128]
@@ -506,53 +540,50 @@
         gblocks_ref[1, p, 64:80, :] = jnp.where(low16, pltpu.roll(pos, 64, 1), 0.0).astype(BF16)
 
 
-def landed_block(copies, landed, i):
-    copies[i].wait_recv()
-    return landed[i].astype(F32)
-
-
-def return_kernel(
-    dom_size,
-    gblocks_ref, gown_ref, gmap_ref, wup_ref,
-    force_ref, fgrad_ref,
-    matebuf, sendblk, landed, part, heard, send_sem, recv_sem,
-):
-    me = lax.axis_index("dom")
-    quarter = lax.axis_index("edge")
-    core = lax.rem(quarter, 2)
-    mate = quarter + 1 - 2 * core
-    barrier = greet(dom_size)
-    pl.semaphore_wait(barrier, NOFF + QUART - 1)
-    share = pltpu.make_async_remote_copy(
+    pool = pltpu.make_async_remote_copy(
         src_ref=gblocks_ref.at[1 - core],
         dst_ref=matebuf,
-        send_sem=send_sem.at[PAIRS + QUART - 1],
-        recv_sem=recv_sem.at[PAIRS + QUART - 1],
+        send_sem=back_send_sem.at[PAIRS + QUART - 1],
+        recv_sem=back_recv_sem.at[PAIRS + QUART - 1],
         device_id=(me, mate),
         device_id_type=MESH,
     )
-    share.start()
-    share.wait_recv()
-    copies = []
+    pool.start()
+
+    def own_spread(step, carry):
+        lanes = pl.ds(pl.multiple_of(step * NE, NE), NE)
+        scat[0 : 2 * GROWS, :] += mm_nt(masked(step, lanes, range(2)), hot_s[:, lanes])
+        return carry
+
+    lax.fori_loop(0, STEPS // 2, own_spread, 0)
+    pool.wait_recv()
+    backs = []
     for i in range(PAIRS):
-        sendblk[i] = (gblocks_ref[core, i].astype(F32) + matebuf[i].astype(F32)).astype(BF16)
+        backblk[i] = (gblocks_ref[core, i].astype(F32) + matebuf[i].astype(F32)).astype(BF16)
         copy = pltpu.make_async_remote_copy(
-            src_ref=sendblk.at[i],
+            src_ref=backblk.at[i],
             dst_ref=landed.at[i],
-            send_sem=send_sem.at[i],
-            recv_sem=recv_sem.at[i],
+            send_sem=back_send_sem.at[i],
+            recv_sem=back_recv_sem.at[i],
             device_id=offset_device(dom_size, i, core, -1),
             device_id_type=MESH,
         )
         copy.start()
-        copies.append(copy)
-
-    low = iota((64, 128), 1) < 64
-    low16 = iota((16, 128), 1) < 64
+        backs.append(copy)
+
+    lax.fori_loop(STEPS // 2, STEPS, own_spread, 0)
+    for g in range(2):
+        span = slice(256 * g, 256 * g + 256)
+        gown_ref[0:128, span] = scat[GROWS * g : GROWS * g + 128, :]
+        gown_ref[128:136, span] = (
+            scat[GROWS * g + 128 : GROWS * g + 136, :] + scat[GROWS * g + 136 : GROWS * g + 144, :]
+        )
+    gown_ref[128:136, mine] = gown_ref[128:136, mine] - down
+
     total = jnp.zeros((GROWS, ATOMS), F32)
     for i in range(0, PAIRS, 2):
-        even = landed_block(copies, landed, i)
-        odd = landed_block(copies, landed, i + 1) if i + 1 < PAIRS else jnp.zeros((BLK, 128), F32)
+        even = landed_block(backs, landed, i)
+        odd = landed_block(backs, landed, i + 1) if i + 1 < PAIRS else jnp.zeros((BLK, 128), F32)
         top = jnp.where(low, even[0:64], pltpu.roll(odd[0:64], 64, 1))
         bottom = jnp.where(low, pltpu.roll(even[0:64], 64, 1), odd[0:64])
         pos = jnp.where(low16, even[64:80], pltpu.roll(odd[64:80], 64, 1))
@@ -572,8 +603,8 @@
         copy = pltpu.make_async_remote_copy(
             src_ref=part.at[peer],
             dst_ref=heard.at[j - 1],
-            send_sem=send_sem.at[PAIRS + j - 1],
-            recv_sem=recv_sem.at[PAIRS + j - 1],
+            send_sem=back_send_sem.at[PAIRS + j - 1],
+            recv_sem=back_recv_sem.at[PAIRS + j - 1],
             device_id=(me, peer),
             device_id_type=MESH,
         )
@@ -583,15 +614,8 @@
     for j, copy in enumerate(sums):
         copy.wait_recv()
         got = got + heard[j]
-    force_ref[...] = -got[128:131]
-    fgrad_ref[...] = lax.dot_general(
-        got[0:128].T,
-        wup_ref[...].astype(F32),
-        (((1,), (1,)), ((), ())),
-        precision=HIGH,
-        preferred_element_type=F32,
-    )
-    for copy in copies + sums + [share]:
+    grad_ref[...] = got
+    for copy in backs + sums + [pool]:
         copy.wait_send()
 
 
@@ -604,7 +628,9 @@
         in_specs=[VMEM_SPEC] * 10,
         out_specs=(VMEM_SPEC,) * 3,
         scratch_shapes=[
-            pltpu.VMEM((GROUPS * GROWS, 256), BF16),
+            pltpu.VMEM((TROWS, 256), BF16),
+            pltpu.VMEM((TROWS, 256), F32),
+            pltpu.VMEM((CH, edge_total), BF16),
             pltpu.VMEM((256, edge_total), BF16),
             pltpu.VMEM((9 * CH, OWN), F32),
             pltpu.VMEM((3 * CH, edge_total), F32),
@@ -628,39 +654,59 @@
     )(*operands)
 
 
-def exchange_call(dom_size, *operands):
+def finish_kernel(energy_ref, grad_ref, wup_ref, energy_out, force_out, fgrad_out):
+    energy_out[...] = energy_ref[...]
+    force_out[...] = -grad_ref[128:131, :]
+    fgrad_out[...] = lax.dot_general(
+        grad_ref[0:128, :].T,
+        wup_ref[...].astype(F32),
+        (((1,), (1,)), ((), ())),
+        precision=HIGH,
+        preferred_element_type=F32,
+    )
+
+
+def interaction_call(dom_size, *operands):
     sds = jax.ShapeDtypeStruct
     edges = QUART * EDGE_ROWS
+    edge_total = OWN * RANKS
     return pl.pallas_call(
-        lambda *refs: exchange_kernel(dom_size, *refs),
-        out_shape=(sds((RANKS, OWN), I32), sds((2, PAIRS, BLK, 128), BF16), sds((CH, ATOMS), BF16)),
-        in_specs=[VMEM_SPEC] * 6 + [pl.BlockSpec(memory_space=pltpu.SMEM)],
-        out_specs=(VMEM_SPEC,) * 3,
+        lambda *refs: interaction_kernel(dom_size, *refs),
+        out_shape=(sds((1, OWN), F32), sds((136, OWN), F32)),
+        in_specs=[VMEM_SPEC] * 6 + [pl.BlockSpec(memory_space=pltpu.SMEM)] + [VMEM_SPEC] * 6,
+        out_specs=(VMEM_SPEC,) * 2,
         scratch_shapes=[
+            pltpu.VMEM((RANKS, OWN), I32),
+            pltpu.VMEM((2, PAIRS, BLK, 128), BF16),
+            pltpu.VMEM((CH, ATOMS), BF16),
+            pltpu.VMEM((2, PAIRS, BLK, 128), BF16),
+            pltpu.VMEM((136, ATOMS), F32),
             pltpu.VMEM((PAIRS, BLK, 128), BF16),
             pltpu.VMEM((QUART, EDGE_ROWS, 128), I32),
             pltpu.VMEM((edges, 128), F32),
             pltpu.VMEM((edges, 128), F32),
             pltpu.VMEM((edges, 128), F32),
             pltpu.VMEM((256, 384), BF16),
-            pltpu.SemaphoreType.DMA((PAIRS + QUART,)),
-            pltpu.SemaphoreType.DMA((PAIRS + QUART,)),
-        ],
-        compiler_params=pltpu.CompilerParams(
-            collective_id=0, has_side_effects=True, vmem_limit_bytes=LIMIT
-        ),
-        name="exchange",
-    )(*operands)
-
-
-def giveback_call(dom_size, *operands):
-    sds = jax.ShapeDtypeStruct
-    return pl.pallas_call(
-        lambda *refs: return_kernel(dom_size, *refs),
-        out_shape=(sds((3, OWN), F32), sds((OWN, CH), F32)),
-        in_specs=[VMEM_SPEC] * 4,
-        out_specs=(VMEM_SPEC,) * 2,
-        scratch_shapes=[
+            pltpu.VMEM((TROWS, 256), BF16),
+            pltpu.VMEM((TROWS, 256), F32),
+            pltpu.VMEM((GROWS, edge_total), BF16),
+            pltpu.VMEM((256, edge_total), BF16),
+            pltpu.VMEM((9 * CH, OWN), F32),
+            pltpu.VMEM((3 * CH, edge_total), F32),
+            pltpu.VMEM((CH, edge_total), F32),
+            pltpu.VMEM((64, edge_total), F32),
+            pltpu.VMEM((64, edge_total), F32),
+            pltpu.VMEM((8, edge_total), F32),
+            pltpu.VMEM((8, edge_total), F32),
+            pltpu.VMEM((GROUPS * GROWS, 256), F32),
+            pltpu.VMEM((128, 128), F32),
+            pltpu.VMEM((64, 24), BF16),
+            pltpu.VMEM((64, 192), BF16),
+            pltpu.VMEM((384, 192), BF16),
+            pltpu.VMEM((8, 192), BF16),
+            pltpu.VMEM((64, 192), BF16),
+            pltpu.VMEM((128, 384), BF16),
+            pltpu.VMEM((24, NE), F32),
             pltpu.VMEM((PAIRS, BLK, 128), BF16),
             pltpu.VMEM((PAIRS, BLK, 128), BF16),
             pltpu.VMEM((PAIRS, BLK, 128), BF16),
@@ -668,11 +714,13 @@
             pltpu.VMEM((QUART - 1, 136, 128), F32),
             pltpu.SemaphoreType.DMA((PAIRS + QUART,)),
             pltpu.SemaphoreType.DMA((PAIRS + QUART,)),
+            pltpu.SemaphoreType.DMA((PAIRS + QUART,)),
+            pltpu.SemaphoreType.DMA((PAIRS + QUART,)),
         ],
         compiler_params=pltpu.CompilerParams(
-            collective_id=1, has_side_effects=True, vmem_limit_bytes=LIMIT
+            collective_id=0, has_side_effects=True, vmem_limit_bytes=LIMIT
         ),
-        name="giveback",
+        name="interaction",
     )(*operands)
 
 
@@ -680,15 +728,19 @@
     dom_size, coordinates, features, species, ghost_map, edge_sender, edge_receiver, edge_count,
     w_up, radial_one, radial_two, radial_three, read_mix, species_out,
 ):
-    slots, blocks, own = exchange_call(
+    sds = jax.ShapeDtypeStruct
+    energy, grad = interaction_call(
         dom_size, features, w_up, coordinates, ghost_map,
         edge_sender.reshape(EDGE_ROWS, 128), edge_receiver.reshape(EDGE_ROWS, 128), edge_count,
+        species.reshape(QUART, OWN), radial_one, radial_two, radial_three, read_mix, species_out,
     )
-    energy, gblocks, gown = compute_call(
-        slots, blocks, own, coordinates, species.reshape(QUART, OWN),
-        radial_one, radial_two, radial_three, read_mix, species_out,
-    )
-    forces, feature_grad = giveback_call(dom_size, gblocks, gown, ghost_map, w_up)
+    energy, forces, feature_grad = pl.pallas_call(
+        finish_kernel,
+        out_shape=(sds((1, OWN), F32), sds((3, OWN), F32), sds((OWN, CH), F32)),
+        in_specs=[VMEM_SPEC] * 3,
+        out_specs=(VMEM_SPEC,) * 3,
+        name="finish",
+    )(energy, grad, w_up)
     return energy.reshape(OWN), forces, feature_grad
 
 

time: 86.2 us -> 76.4 us (0.89)
  Pallas kernels: 81.8 us -> 74.9 us
  local copies, waits for them, and re-layouts: 2.71 us -> 0 us
    pallas_call x3 -> x2, Pallas kernels: 81.8 us -> 74.9 us  [the longest x1 73.1 us: interaction_call(): pl.pallas_call(lambda *refs: interaction_kernel(dom_size, *refs), out_sha...]
    unnamed x4 -> x0, local copies, waits for them, and re-layouts: 2.71 us -> none
where the time goes in v3:
time: 76.4 us; the launch traced here: 76.2 us
  Pallas kernels  74.9 us (98%)
  between operations  1.29 us (2%)
    pallas_call x1, Pallas kernels, interaction_call(): pl.pallas_call(lambda *refs: interaction_kernel(dom_size, *refs), out_sha...  73.1 us
    pallas_call x1, Pallas kernels, on_device(): pl.pallas_call(finish_kernel, out_shape=(sds((1, OWN), F32), sds((3, OWN)...  1.79 us

profile of v3, /device:TPU:3, one launch (start us, length us, event | category | flops | bytes accessed | tf_op | source)
XLA Modules:
  0.0 76.2 jit_solution(3243960389822403665)
XLA Ops:
  1.3 73.1 %interaction.1 = (f32[1,128]{1,0:T(1,128)}, f32[136,128]{1,0:T(8,128)}) custom-call(bf16[512,128]{1,0:T(8,128)(2,1)} %refs_0_.1, bf16[128,128]{1,0:T(8,128)(2,1)} %wup_ref.1, bf16[3,512]{1,0:T(4,128)(2,1)} %refs_2_.1, s32[26,64]{1,0:T(8,128)} %refs_3_.1, s32[64,128]{1,0:T(8,128)} %bitcast.4, s32[64,128]{1,0:T(8,128)} %bitcast.5, s32[1]{0:T(128)S(6)} %copy.16.refs_6_, ...), custom_call_target="tpu_custom_call" | custom-call | tf_op jit(solution)/shard_map/interaction/pallas_call | solution.py:673
  74.4 1.8 %finish.1 = (f32[1,128]{1,0:T(1,128)}, f32[3,128]{1,0:T(4,128)}, f32[128,128]{1,0:T(8,128)}) custom-call(f32[1,128]{1,0:T(1,128)} %get-tuple-element.8.energy_ref, f32[136,128]{1,0:T(8,128)} %get-tuple-element.9.grad_ref, bf16[128,128]{1,0:T(8,128)(2,1)} %wup_ref.1), custom_call_target="tpu_custom_call" | custom-call | tf_op jit(solution)/shard_map/finish/pallas_call | solution.py:737

commit v4 on v3

--- a/solution.py
+++ b/solution.py
@@ -25,7 +25,6 @@
 PER = 16
 NE = PER * OWN
 STEPS = OWN * RANKS // NE
-SORT_ROWS = 64
 BLK = 80
 SENTINEL = 4095
 LIMIT = 56 * 1024 * 1024
@@ -37,6 +36,9 @@
     for c in (-1, 0, 1)
     if (a, b, c) != (0, 0, 0)
 ]
+
+
+SEND_ORDER = sorted(range(PAIRS), key=lambda i: -abs(2 * i - PAIRS + 1))
 
 
 def shifts(count):
@@ -128,9 +130,9 @@
     w1_ref, w2_ref, w3_ref, mix_ref, sp_ref,
     energy_ref, grad_ref,
     slots_ref, blocks_ref, own_ref, gblocks_ref, gown_ref,
-    sendblk, epack, li_s, g_s, hi_s, tri_s,
+    sendblk, epack, tri_s,
     tab, tab32, dh_s, hot_s, acc, rad_s, h_s, d1_s, d2_s, bas_s, row_s, scat, sp_s,
-    w1f, w2f, w3f, w1b, w2b, w3b, myc,
+    w1f, w2f, w3f, w1b, w2b, w3b, myc, mix_t, kind_s,
     matebuf, backblk, landed, part, heard, send_sem, recv_sem, back_send_sem, back_recv_sem,
 ):
     me = lax.axis_index("dom")
@@ -182,8 +184,8 @@
         copy.start()
         copies.append(copy)
 
-    ghosts = []
-    for j in range(PAIRS):
+    ghosts = [None] * PAIRS
+    for j in SEND_ORDER:
         copy = pltpu.make_async_remote_copy(
             src_ref=sendblk.at[j],
             dst_ref=blocks_ref.at[core, j],
@@ -193,7 +195,7 @@
             device_id_type=MESH,
         )
         copy.start()
-        ghosts.append(copy)
+        ghosts[j] = copy
 
     coords = coord_ref[...].astype(F32)
     coords8 = jnp.concatenate([coords, jnp.zeros((5, ATOMS), F32)], axis=0)
@@ -228,36 +230,35 @@
 
     sp_s[...] = jnp.zeros((128, 128), F32)
     sp_s[0:89, :] = sp_ref[...]
-
-    for copy in copies:
-        copy.wait_recv()
-
-    packed = epack[...].reshape(QUART * EDGE_ROWS, 128)
-    local = (packed >> 16) - quarter * OWN
-    inside = (local >= 0) & (local < OWN)
-    li_s[...] = jnp.where(inside, local, 255).astype(F32)
-    value = packed & 65535
-    g_s[...] = (value >> 8).astype(F32)
-    hi_s[...] = (value & 255).astype(F32)
+    kinds = species_ref[pl.ds(quarter, 1), :]
+    kind_hot = jnp.where(iota((128, 128), 0) == kinds, 1.0, 0.0)
+    kind_s[...] = mm_high(sp_s[...].T, kind_hot)
+    mix_t[...] = mix_ref[...].T
+
     tri_s[:, 0:256] = jnp.where(iota((256, 256), 0) < iota((256, 256), 1), 1.0, 0.0).astype(BF16)
     tri_s[:, 256:384] = jnp.ones((256, 128), BF16)
 
     atom = iota((OWN, 256), 0).astype(F32)
     rank_of = iota((RANKS, 256), 0).astype(F32)
 
-    def sort_step(step, carry):
+    def sort_quarter(source, carry):
         base, total = carry
-        rows = pl.ds(pl.multiple_of(step * SORT_ROWS, SORT_ROWS), SORT_ROWS)
-        li8, g8, hi8 = li_s[rows, :], g_s[rows, :], hi_s[rows, :]
+        packed = epack[source]
+        local = (packed >> 16) - quarter * OWN
+        inside = (local >= 0) & (local < OWN)
+        li8 = jnp.where(inside, local, 255).astype(F32)
+        value = packed & 65535
+        g8 = (value >> 8).astype(F32)
+        hi8 = (value & 255).astype(F32)
 
         def lane_row(x, b):
             return jnp.concatenate([x[2 * b : 2 * b + 1], x[2 * b + 1 : 2 * b + 2]], axis=1)
 
-        hots = [jnp.where(atom == lane_row(li8, b), 1.0, 0.0) for b in range(SORT_ROWS // 2)]
+        hots = [jnp.where(atom == lane_row(li8, b), 1.0, 0.0) for b in range(EDGE_ROWS // 2)]
         hots16 = [hot.astype(BF16) for hot in hots]
         counts = mm(jnp.concatenate(hots16, axis=0), tri_s[...])
         lefts = []
-        for b in range(SORT_ROWS // 2):
+        for b in range(EDGE_ROWS // 2):
             block = counts[OWN * b : OWN * (b + 1)]
             before = block[:, 0:256] + jnp.concatenate([base, base], axis=1)
             base = base + block[:, 256:384]
@@ -276,8 +277,10 @@
         return base, total
 
     zero = jnp.zeros((OWN, 128), F32)
-    steps = QUART * EDGE_ROWS // SORT_ROWS
-    state = lax.fori_loop(0, steps // 2, sort_step, (zero, zero))
+    state = sort_quarter(quarter, (zero, zero))
+    for j in (1, 2):
+        copies[j - 1].wait_recv()
+        state = sort_quarter(lax.rem(quarter + QUART - j, QUART), state)
     for copy in ghosts:
         copy.wait_recv()
     share = pltpu.make_async_remote_copy(
@@ -289,7 +292,8 @@
         device_id_type=MESH,
     )
     share.start()
-    _, total = lax.fori_loop(steps // 2, steps, sort_step, state)
+    copies[2].wait_recv()
+    _, total = sort_quarter(lax.rem(quarter + QUART - 3, QUART), state)
     slots_ref[...] = (total[0:64] * 256.0 + total[64:128]).astype(I32)
     share.wait_recv()
     for copy in copies + ghosts + [share]:
@@ -416,12 +420,10 @@
     cz = xz * vx + yz * vy + zz * vz
     cub = cx * vx + cy * vy + cz * vz
     inv = jnp.concatenate([a0, n1, n2, a0 * n1, cub], axis=0)
-    pre = mm_high(mix_ref[...].T, inv)
+    pre = mm_high(mix_t[...], inv)
     sig = 0.5 + 0.5 * jnp.tanh(0.5 * pre)
     hid = pre * sig
-    kinds = species_ref[pl.ds(quarter, 1), :]
-    kind_hot = jnp.where(iota((128, 128), 0) == kinds, 1.0, 0.0)
-    per_kind = mm_high(sp_s[...].T, kind_hot)
+    per_kind = kind_s[...]
     energy_ref[...] = jnp.sum(hid * per_kind, axis=0, keepdims=True)
     dpre = per_kind * (sig + hid * (1.0 - sig))
     dinv = mm_high(mix_ref[...], dpre) * 0.125
@@ -557,8 +559,8 @@
 
     lax.fori_loop(0, STEPS // 2, own_spread, 0)
     pool.wait_recv()
-    backs = []
-    for i in range(PAIRS):
+    backs = [None] * PAIRS
+    for i in SEND_ORDER:
         backblk[i] = (gblocks_ref[core, i].astype(F32) + matebuf[i].astype(F32)).astype(BF16)
         copy = pltpu.make_async_remote_copy(
             src_ref=backblk.at[i],
@@ -569,7 +571,7 @@
             device_id_type=MESH,
         )
         copy.start()
-        backs.append(copy)
+        backs[i] = copy
 
     lax.fori_loop(STEPS // 2, STEPS, own_spread, 0)
     for g in range(2):
@@ -619,41 +621,6 @@
         copy.wait_send()
 
 
-def compute_call(*operands):
-    sds = jax.ShapeDtypeStruct
-    edge_total = OWN * RANKS
-    return pl.pallas_call(
-        compute_kernel,
-        out_shape=(sds((1, OWN), F32), sds((2, PAIRS, BLK, 128), BF16), sds((136, ATOMS), F32)),
-        in_specs=[VMEM_SPEC] * 10,
-        out_specs=(VMEM_SPEC,) * 3,
-        scratch_shapes=[
-            pltpu.VMEM((TROWS, 256), BF16),
-            pltpu.VMEM((TROWS, 256), F32),
-            pltpu.VMEM((CH, edge_total), BF16),
-            pltpu.VMEM((256, edge_total), BF16),
-            pltpu.VMEM((9 * CH, OWN), F32),
-            pltpu.VMEM((3 * CH, edge_total), F32),
-            pltpu.VMEM((CH, edge_total), F32),
-            pltpu.VMEM((64, edge_total), F32),
-            pltpu.VMEM((64, edge_total), F32),
-            pltpu.VMEM((8, edge_total), F32),
-            pltpu.VMEM((8, edge_total), F32),
-            pltpu.VMEM((GROUPS * GROWS, 256), F32),
-            pltpu.VMEM((128, 128), F32),
-            pltpu.VMEM((64, 24), BF16),
-            pltpu.VMEM((64, 192), BF16),
-            pltpu.VMEM((384, 192), BF16),
-            pltpu.VMEM((8, 192), BF16),
-            pltpu.VMEM((64, 192), BF16),
-            pltpu.VMEM((128, 384), BF16),
-            pltpu.VMEM((24, NE), F32),
-        ],
-        compiler_params=pltpu.CompilerParams(vmem_limit_bytes=LIMIT),
-        name="compute",
-    )(*operands)
-
-
 def finish_kernel(energy_ref, grad_ref, wup_ref, energy_out, force_out, fgrad_out):
     energy_out[...] = energy_ref[...]
     force_out[...] = -grad_ref[128:131, :]
@@ -668,7 +635,6 @@
 
 def interaction_call(dom_size, *operands):
     sds = jax.ShapeDtypeStruct
-    edges = QUART * EDGE_ROWS
     edge_total = OWN * RANKS
     return pl.pallas_call(
         lambda *refs: interaction_kernel(dom_size, *refs),
@@ -683,9 +649,6 @@
             pltpu.VMEM((136, ATOMS), F32),
             pltpu.VMEM((PAIRS, BLK, 128), BF16),
             pltpu.VMEM((QUART, EDGE_ROWS, 128), I32),
-            pltpu.VMEM((edges, 128), F32),
-            pltpu.VMEM((edges, 128), F32),
-            pltpu.VMEM((edges, 128), F32),
             pltpu.VMEM((256, 384), BF16),
             pltpu.VMEM((TROWS, 256), BF16),
             pltpu.VMEM((TROWS, 256), F32),
@@ -707,6 +670,8 @@
             pltpu.VMEM((64, 192), BF16),
             pltpu.VMEM((128, 384), BF16),
             pltpu.VMEM((24, NE), F32),
+            pltpu.VMEM((128, 5 * CH), F32),
+            pltpu.VMEM((128, OWN), F32),
             pltpu.VMEM((PAIRS, BLK, 128), BF16),
             pltpu.VMEM((PAIRS, BLK, 128), BF16),
             pltpu.VMEM((PAIRS, BLK, 128), BF16),

time: 76.4 us -> 75.3 us (0.986)
  Pallas kernels: 74.9 us -> 73.8 us
    pallas_call x1, Pallas kernels: 73.1 us -> 72 us  [interaction_call(): pl.pallas_call(lambda *refs: interaction_kernel(dom_size, *refs), out_sha...]
where the time goes in v4:
time: 75.3 us; the launch traced here: 75.1 us
  Pallas kernels  73.8 us (98%)
  between operations  1.29 us (2%)
    pallas_call x1, Pallas kernels, interaction_call(): pl.pallas_call(lambda *refs: interaction_kernel(dom_size, *refs), out_sha...  72 us
    pallas_call x1, Pallas kernels, on_device(): pl.pallas_call(finish_kernel, out_shape=(sds((1, OWN), F32), sds((3, OWN)...  1.79 us

profile of v4, /device:TPU:3, one launch (start us, length us, event | category | flops | bytes accessed | tf_op | source)
XLA Modules:
  0.0 75.1 jit_solution(2659665789099700826)
XLA Ops:
  1.3 72.0 %interaction.1 = (f32[1,128]{1,0:T(1,128)}, f32[136,128]{1,0:T(8,128)}) custom-call(bf16[512,128]{1,0:T(8,128)(2,1)} %refs_0_.1, bf16[128,128]{1,0:T(8,128)(2,1)} %wup_ref.1, bf16[3,512]{1,0:T(4,128)(2,1)} %refs_2_.1, s32[26,64]{1,0:T(8,128)} %refs_3_.1, s32[64,128]{1,0:T(8,128)} %bitcast.4, s32[64,128]{1,0:T(8,128)} %bitcast.5, s32[1]{0:T(128)S(6)} %copy.16.refs_6_, ...), custom_call_target="tpu_custom_call" | custom-call | tf_op jit(solution)/shard_map/interaction/pallas_call | solution.py:639
  73.3 1.8 %finish.1 = (f32[1,128]{1,0:T(1,128)}, f32[3,128]{1,0:T(4,128)}, f32[128,128]{1,0:T(8,128)}) custom-call(f32[1,128]{1,0:T(1,128)} %get-tuple-element.8.energy_ref, f32[136,128]{1,0:T(8,128)} %get-tuple-element.9.grad_ref, bf16[128,128]{1,0:T(8,128)(2,1)} %wup_ref.1), custom_call_target="tpu_custom_call" | custom-call | tf_op jit(solution)/shard_map/finish/pallas_call | solution.py:702

commit v5 on v4

--- a/solution.py
+++ b/solution.py
@@ -25,8 +25,10 @@
 PER = 16
 NE = PER * OWN
 STEPS = OWN * RANKS // NE
+SORT_ROWS = 64
 BLK = 80
 SENTINEL = 4095
+PARTS = ([7, 8], [5, 6], [3, 4], [2])
 LIMIT = 56 * 1024 * 1024
 
 OFFSETS = [
@@ -133,7 +135,7 @@
     sendblk, epack, tri_s,
     tab, tab32, dh_s, hot_s, acc, rad_s, h_s, d1_s, d2_s, bas_s, row_s, scat, sp_s,
     w1f, w2f, w3f, w1b, w2b, w3b, myc, mix_t, kind_s,
-    matebuf, backblk, landed, part, heard, send_sem, recv_sem, back_send_sem, back_recv_sem,
+    matebuf, backblk, landed, sums_s, heard, send_sem, recv_sem, back_send_sem, back_recv_sem,
 ):
     me = lax.axis_index("dom")
     quarter = lax.axis_index("edge")
@@ -241,9 +243,30 @@
     atom = iota((OWN, 256), 0).astype(F32)
     rank_of = iota((RANKS, 256), 0).astype(F32)
 
-    def sort_quarter(source, carry):
+    share = pltpu.make_async_remote_copy(
+        src_ref=blocks_ref.at[core],
+        dst_ref=blocks_ref.at[core],
+        send_sem=send_sem.at[PAIRS + QUART - 1],
+        recv_sem=recv_sem.at[PAIRS + QUART - 1],
+        device_id=(me, mate),
+        device_id_type=MESH,
+    )
+
+    def sort_step(step, carry):
         base, total = carry
-        packed = epack[source]
+        for j in range(1, QUART):
+
+            @pl.when(step == j)
+            def _():
+                copies[j - 1].wait_recv()
+
+        @pl.when(step == QUART - 1)
+        def _():
+            for copy in ghosts:
+                copy.wait_recv()
+            share.start()
+
+        packed = epack[lax.rem(quarter + QUART - step, QUART)]
         local = (packed >> 16) - quarter * OWN
         inside = (local >= 0) & (local < OWN)
         li8 = jnp.where(inside, local, 255).astype(F32)
@@ -254,11 +277,11 @@
         def lane_row(x, b):
             return jnp.concatenate([x[2 * b : 2 * b + 1], x[2 * b + 1 : 2 * b + 2]], axis=1)
 
-        hots = [jnp.where(atom == lane_row(li8, b), 1.0, 0.0) for b in range(EDGE_ROWS // 2)]
+        hots = [jnp.where(atom == lane_row(li8, b), 1.0, 0.0) for b in range(SORT_ROWS // 2)]
         hots16 = [hot.astype(BF16) for hot in hots]
         counts = mm(jnp.concatenate(hots16, axis=0), tri_s[...])
         lefts = []
-        for b in range(EDGE_ROWS // 2):
+        for b in range(SORT_ROWS // 2):
             block = counts[OWN * b : OWN * (b + 1)]
             before = block[:, 0:256] + jnp.concatenate([base, base], axis=1)
             base = base + block[:, 256:384]
@@ -277,23 +300,7 @@
         return base, total
 
     zero = jnp.zeros((OWN, 128), F32)
-    state = sort_quarter(quarter, (zero, zero))
-    for j in (1, 2):
-        copies[j - 1].wait_recv()
-        state = sort_quarter(lax.rem(quarter + QUART - j, QUART), state)
-    for copy in ghosts:
-        copy.wait_recv()
-    share = pltpu.make_async_remote_copy(
-        src_ref=blocks_ref.at[core],
-        dst_ref=blocks_ref.at[core],
-        send_sem=send_sem.at[PAIRS + QUART - 1],
-        recv_sem=recv_sem.at[PAIRS + QUART - 1],
-        device_id=(me, mate),
-        device_id_type=MESH,
-    )
-    share.start()
-    copies[2].wait_recv()
-    _, total = sort_quarter(lax.rem(quarter + QUART - 3, QUART), state)
+    _, total = lax.fori_loop(0, QUART * EDGE_ROWS // SORT_ROWS, sort_step, (zero, zero))
     slots_ref[...] = (total[0:64] * 256.0 + total[64:128]).astype(I32)
     share.wait_recv()
     for copy in copies + ghosts + [share]:
@@ -440,13 +447,12 @@
     acc[896:1024, :] = 2.0 * g2 * (xx - zz) + g4 * (vx * vx - vz * vz)
     acc[1024:1152, :] = 2.0 * g2 * (yy - zz) + g4 * (vy * vy - vz * vz)
 
-    def edge_grads(step, lanes, _):
+    def grads_part(lanes, part, state):
         x, y, z, dsq, env, _ = row_values(lanes)
         ys = harmonic(x, y, z, dsq)
-        denv = jnp.zeros((8, NE), F32)
-        dys = [jnp.zeros((8, NE), F32) for _ in range(9)]
-        dhs, drs = [], [[], [], []]
-        for t in range(16):
+        denv, dys, drs = state
+        dhs = []
+        for t in range(4 * part, 4 * part + 4):
             da = []
             for m in range(9):
                 v = acc[128 * m + 8 * t : 128 * m + 8 * t + 8, :]
@@ -468,10 +474,8 @@
             d1, d2 = he * rs[1], he * rs[2]
             for m in range(1, 9):
                 dys[m] = dys[m] + (d1 if m < 4 else d2) * da[m]
-        drad = jnp.concatenate(drs[0] + drs[1] + drs[2], axis=0).astype(BF16)
-        both = mm(w3b[...], drad)
-        dh_s[0:128, lanes] = jnp.concatenate(dhs, axis=0).astype(BF16)
-        return denv, dys, both
+        dh_s[32 * part : 32 * part + 32, lanes] = jnp.concatenate(dhs, axis=0).astype(BF16)
+        return denv, dys, drs
 
     def radial_back_two(step, lanes, given):
         denv, dys, both = given
@@ -512,17 +516,30 @@
             lefts.extend(dh_s[16 * t : 16 * t + 16, lanes] * mask for t in range(GROWS // 16))
         return jnp.concatenate(lefts, axis=0)
 
-    def spread(step, lanes, drel):
-        drel_hi = drel.astype(BF16).astype(F32)
-        dh_s[128:144, lanes] = jnp.concatenate([drel_hi, drel - drel_hi], axis=0).astype(BF16)
-        scat[2 * GROWS :, :] += mm_nt(masked(step, lanes, range(2, GROUPS)), hot_s[:, lanes])
-        return fold(drel)
-
-    def bwd(step, down):
-        stages = [edge_grads, radial_back_two, radial_back_one, position_grads, spread]
-        return down + staged(stages, step)
-
-    down = lax.fori_loop(0, STEPS, bwd, jnp.zeros((8, 128), F32))
+    def spread_part(step, lanes, groups):
+        span = slice(GROWS * groups[0], GROWS * groups[-1] + GROWS)
+        scat[span, :] += mm_nt(masked(step, lanes, groups), hot_s[:, lanes])
+
+    down = jnp.zeros((8, 128), F32)
+    for step in range(STEPS + 1):
+        ahead = step < STEPS
+        if ahead:
+            lanes = slice(step * NE, step * NE + NE)
+            state = jnp.zeros((8, NE), F32), [jnp.zeros((8, NE), F32) for _ in range(9)], [[], [], []]
+        for part in range(4):
+            if step > 0:
+                spread_part(step - 1, slice(step * NE - NE, step * NE), PARTS[part])
+            if ahead:
+                state = grads_part(lanes, part, state)
+        if ahead:
+            denv, dys, drs = state
+            drad = jnp.concatenate(drs[0] + drs[1] + drs[2], axis=0).astype(BF16)
+            given = radial_back_two(step, lanes, (denv, dys, mm(w3b[...], drad)))
+            given = radial_back_one(step, lanes, given)
+            drel = position_grads(step, lanes, given)
+            drel_hi = drel.astype(BF16).astype(F32)
+            dh_s[128:144, lanes] = jnp.concatenate([drel_hi, drel - drel_hi], axis=0).astype(BF16)
+            down = down + fold(drel)
 
     for p in range(PAIRS):
         g, at = 2 + p // 2, 128 * (p % 2)
@@ -596,14 +613,14 @@
     pos = total[128:136] + total[136:144] + gown_ref[128:136, :]
     for j in range(QUART):
         span = slice(128 * j, 128 * j + 128)
-        part[j, 0:128, :] = feat[:, span]
-        part[j, 128:136, :] = pos[:, span]
+        sums_s[j, 0:128, :] = feat[:, span]
+        sums_s[j, 128:136, :] = pos[:, span]
 
     sums = []
     for j in range(1, QUART):
         peer = lax.rem(quarter + j, QUART)
         copy = pltpu.make_async_remote_copy(
-            src_ref=part.at[peer],
+            src_ref=sums_s.at[peer],
             dst_ref=heard.at[j - 1],
             send_sem=back_send_sem.at[PAIRS + j - 1],
             recv_sem=back_recv_sem.at[PAIRS + j - 1],
@@ -612,7 +629,7 @@
         )
         copy.start()
         sums.append(copy)
-    got = part[quarter]
+    got = sums_s[quarter]
     for j, copy in enumerate(sums):
         copy.wait_recv()
         got = got + heard[j]

time: 75.3 us -> 72 us (0.956)
  Pallas kernels: 73.8 us -> 70.5 us
    pallas_call x1, Pallas kernels: 72 us -> 68.7 us  [interaction_call(): pl.pallas_call(lambda *refs: interaction_kernel(dom_size, *refs), out_sha...]
where the time goes in v5:
time: 72 us; the launch traced here: 71.8 us
  Pallas kernels  70.5 us (98%)
  between operations  1.29 us (2%)
    pallas_call x1, Pallas kernels, interaction_call(): pl.pallas_call(lambda *refs: interaction_kernel(dom_size, *refs), out_sha...  68.7 us
    pallas_call x1, Pallas kernels, on_device(): pl.pallas_call(finish_kernel, out_shape=(sds((1, OWN), F32), sds((3, OWN)...  1.79 us

profile of v5, /device:TPU:3, one launch (start us, length us, event | category | flops | bytes accessed | tf_op | source)
XLA Modules:
  0.0 71.8 jit_solution(8845971496291026052)
XLA Ops:
  1.3 68.7 %interaction.1 = (f32[1,128]{1,0:T(1,128)}, f32[136,128]{1,0:T(8,128)}) custom-call(bf16[512,128]{1,0:T(8,128)(2,1)} %refs_0_.1, bf16[128,128]{1,0:T(8,128)(2,1)} %wup_ref.1, bf16[3,512]{1,0:T(4,128)(2,1)} %refs_2_.1, s32[26,64]{1,0:T(8,128)} %refs_3_.1, s32[64,128]{1,0:T(8,128)} %bitcast.4, s32[64,128]{1,0:T(8,128)} %bitcast.5, s32[1]{0:T(128)S(6)} %copy.16.refs_6_, ...), custom_call_target="tpu_custom_call" | custom-call | tf_op jit(solution)/shard_map/interaction/pallas_call | solution.py:656
  70.0 1.8 %finish.1 = (f32[1,128]{1,0:T(1,128)}, f32[3,128]{1,0:T(4,128)}, f32[128,128]{1,0:T(8,128)}) custom-call(f32[1,128]{1,0:T(1,128)} %get-tuple-element.8.energy_ref, f32[136,128]{1,0:T(8,128)} %get-tuple-element.9.grad_ref, bf16[128,128]{1,0:T(8,128)(2,1)} %wup_ref.1), custom_call_target="tpu_custom_call" | custom-call | tf_op jit(solution)/shard_map/finish/pallas_call | solution.py:719
